TPU v7x, 128 devices: a whole 4x4x4 slice. The times are simulated.
128 devices in a mesh: seq: 32 (over z, y, core), head: 4 (over x).
Axes of the slice: x: 4, y: 4, z: 4, core: 2. Of those that a mesh axis runs over, the one named last changes fastest.
Arguments:
- hidden_in: bfloat16 [8192, 2048], P('seq', 'head'), may hold values from -6 to 6
- out_grad: bfloat16 [8192, 2048], P('seq', 'head'), may hold values from -6 to 6
- norm_attn: float32 [2048], replicated, may hold values from 0.5 to 1.5
- w_query: bfloat16 [2048, 2048], P('seq', 'head'), may hold values from -0.125 to 0.125
- w_key: bfloat16 [2048, 2048], P('seq', 'head'), may hold values from -0.125 to 0.125
- w_value: bfloat16 [2048, 4096], P('seq', 'head'), may hold values from -0.125 to 0.125
- conv_query: bfloat16 [4, 2048], P(None, 'head'), may hold values from -3 to 3
- conv_key: bfloat16 [4, 2048], P(None, 'head'), may hold values from -3 to 3
- conv_value: bfloat16 [4, 4096], P(None, 'head'), may hold values from -3 to 3
- w_alpha: bfloat16 [2048, 16], P('seq', 'head'), may hold values from -0.125 to 0.125
- w_beta: bfloat16 [2048, 16], P('seq', 'head'), may hold values from -0.125 to 0.125
- log_rate: float32 [16], P('head'), may hold values from -12 to -2
- rate_bias: float32 [16], P('head'), may hold values from -1 to 1
- w_gate_out: bfloat16 [2048, 4096], P('seq', 'head'), may hold values from -0.125 to 0.125
- head_norm: float32 [256], replicated, may hold values from 0.5 to 1.5
- w_out: bfloat16 [4096, 2048], P('head', 'seq'), may hold values from -0.1875 to 0.1875
- norm_mlp: float32 [2048], replicated, may hold values from 0.5 to 1.5
- w_mlp_gate: bfloat16 [2048, 5504], P('seq', 'head'), may hold values from -0.125 to 0.125
- w_mlp_up: bfloat16 [2048, 5504], P('seq', 'head'), may hold values from -0.125 to 0.125
- w_mlp_down: bfloat16 [5504, 2048], P('head', 'seq'), may hold values from -0.15625 to 0.15625
Outputs:
- output: bfloat16 [8192, 2048], P('seq', 'head')
- grad_input: bfloat16 [8192, 2048], P('seq', 'head')
- grad_norm_attn: float32 [2048], replicated
- grad_query: float32 [2048, 2048], P('seq', 'head')
- grad_key: float32 [2048, 2048], P('seq', 'head')
- grad_value: float32 [2048, 4096], P('seq', 'head')
- grad_conv_query: float32 [4, 2048], P(None, 'head')
- grad_conv_key: float32 [4, 2048], P(None, 'head')
- grad_conv_value: float32 [4, 4096], P(None, 'head')
- grad_alpha: float32 [2048, 16], P('seq', 'head')
- grad_beta: float32 [2048, 16], P('seq', 'head')
- grad_log_rate: float32 [16], P('head')
- grad_rate_bias: float32 [16], P('head')
- grad_gate_out: float32 [2048, 4096], P('seq', 'head')
- grad_head_norm: float32 [256], replicated
- grad_out: float32 [4096, 2048], P('head', 'seq')
- grad_norm_mlp: float32 [2048], replicated
- grad_mlp_gate: float32 [2048, 5504], P('seq', 'head')
- grad_mlp_up: float32 [2048, 5504], P('seq', 'head')
- grad_mlp_down: float32 [5504, 2048], P('head', 'seq')
All inputs are finite; a program needn't handle non-finite values.
Results may differ from a plain program's by a relative error of at most 0.038.
Values may be sent and summed in bfloat16 or wider, within the bound.
No kernel may reach another device: no remote copies, remote signals or barrier semaphores. Data moves between devices by JAX's collectives and lax.ppermute only.
A program may use at most 256 MiB of HBM per device.

v0:
```python
from functools import partial

import jax
import jax.numpy as jnp
from jax import lax
from jax.sharding import PartitionSpec as P

BLOCK = 64


EPSILON = 1e-06
EXACT_PRECISION = lax.Precision.HIGHEST


def passed_along(value, axis, steps):
    count = lax.axis_size(axis)
    leading, last = (max(0, -steps), min(count, count - steps))
    return lax.ppermute(value, axis, [(source, source + steps) for source in range(leading, last)])


def prefix(x, axis, combine, identity):
    size, place = (lax.axis_size(axis), lax.axis_index(axis))
    everything = jax.tree.map(
        lambda part, kind: lax.all_gather(part.astype(kind), axis), x, (jnp.bfloat16, jnp.bfloat16)
    )
    start = jax.tree.map(
        lambda part, zero: jnp.broadcast_to(jnp.asarray(zero, part.dtype), part.shape), x, identity
    )

    def step(k, before):
        reached = k < place
        new = combine(
            before, jax.tree.map(lambda part, own: part[k].astype(own.dtype), everything, x)
        )
        return jax.tree.map(lambda a, b: jnp.where(reached, a, b), new, before)

    return lax.fori_loop(0, size, step, start)


def prefix_2(x, axis, combine, identity):
    size, place = (lax.axis_size(axis), lax.axis_index(axis))
    everything = jax.tree.map(
        lambda part, kind: lax.all_gather(part.astype(kind), axis),
        x,
        jax.tree.map(lambda a: jnp.bfloat16 if a.dtype == jnp.float32 else a.dtype, x),
    )
    start = jax.tree.map(
        lambda part, zero: jnp.broadcast_to(jnp.asarray(zero, part.dtype), part.shape), x, identity
    )

    def step(k, before):
        at = size - 1 - k
        reached = at > place
        new = combine(
            before, jax.tree.map(lambda part, own: part[at].astype(own.dtype), everything, x)
        )
        return jax.tree.map(lambda a, b: jnp.where(reached, a, b), new, before)

    return lax.fori_loop(0, size, step, start)


def plain_dot(left_op, right_op):
    return jnp.dot(left_op, right_op, preferred_element_type=jnp.float32)


def dot_last(left_op, right_op):
    return lax.dot_general(
        left_op, right_op, (((1,), (1,)), ((), ())), preferred_element_type=jnp.float32
    )


def dot_first(left_op, right_op):
    return lax.dot_general(
        left_op, right_op, (((0,), (0,)), ((), ())), preferred_element_type=jnp.float32
    )


def rms_gain(rows_in, gain_vec):
    factor = lax.rsqrt(jnp.mean(rows_in * rows_in, axis=-1, keepdims=True) + EPSILON)
    return rows_in * factor * gain_vec


def unit_rows(rows_in):
    return rows_in * lax.rsqrt(jnp.sum(rows_in * rows_in, axis=-1, keepdims=True) + EPSILON)


def combine_maps(earlier, later):
    linear = jnp.einsum("hij,hjk->hik", later[0], earlier[0], precision=EXACT_PRECISION)
    affine = jnp.einsum("hij,hjk->hik", later[0], earlier[1], precision=EXACT_PRECISION) + later[1]
    return (linear, affine)


def mixer_inputs(
    padded_rows, conv_all, alpha_in, beta_in, log_rate, rate_bias, key_dimension, value_size
):
    tap_count = conv_all.shape[0]
    row_count = padded_rows.shape[0] - tap_count + 1
    head_count = log_rate.shape[0]
    key_width = head_count * key_dimension
    conv_out = padded_rows[0:row_count] * conv_all[0]
    for position in range(1, tap_count):
        conv_out = conv_out + padded_rows[position : position + row_count] * conv_all[position]
    conv_out = jax.nn.silu(conv_out)
    queries = unit_rows(
        conv_out[:, :key_width].reshape(row_count, head_count, key_dimension)
    ) * key_dimension ** (-0.5)
    key_rows = unit_rows(
        conv_out[:, key_width : 2 * key_width].reshape(row_count, head_count, key_dimension)
    )
    values = conv_out[:, 2 * key_width :].reshape(row_count, head_count, value_size)
    log_decay = -jnp.exp(log_rate) * jax.nn.softplus(alpha_in + rate_bias)
    return (queries, key_rows, values, log_decay, jax.nn.sigmoid(beta_in))


def block_states(queries, key_rows, values, log_decay, beta_rows, length):
    row_count, head_count, key_dimension = key_rows.shape
    value_size = values.shape[2]
    blocks = row_count // length

    def to_blocks(array_in):
        return jnp.swapaxes(array_in.reshape((blocks, length) + array_in.shape[1:]), 1, 2)

    causal_mask = jnp.tril(jnp.ones((length, length), dtype=bool))
    strict_mask = jnp.tril(jnp.ones((length, length), dtype=bool), -1)
    identity = jnp.eye(length, dtype=jnp.float32)
    square_zero = jnp.zeros((head_count, key_dimension, key_dimension), jnp.float32)
    start_state = jnp.concatenate(
        [
            jnp.broadcast_to(
                jnp.eye(key_dimension, dtype=jnp.float32),
                (head_count, key_dimension, key_dimension),
            ),
            jnp.zeros((head_count, key_dimension, value_size), jnp.float32),
        ],
        -1,
    )

    def advance(running_state, block_in):
        query_portion, key_part, value_part, rate_part, beta_part = block_in
        cumulative = jnp.cumsum(rate_part, axis=-1)
        log_gap = cumulative[:, :, None] - cumulative[:, None, :]
        decay_ratio = jnp.exp(jnp.where(causal_mask, log_gap, 0.0))
        key_gram = jnp.einsum("hck,hdk->hcd", key_part, key_part, precision=EXACT_PRECISION)
        system = identity + beta_part[:, :, None] * jnp.where(
            strict_mask, key_gram * decay_ratio, 0.0
        )
        decay_factor_rows = jnp.exp(cumulative)
        right_side = beta_part[:, :, None] * jnp.concatenate(
            [key_part * decay_factor_rows[:, :, None], value_part], -1
        )
        solved = lax.linalg.triangular_solve(
            system, right_side, left_side=True, lower=True, unit_diagonal=True
        )
        weight_matrix_rows = solved[..., :key_dimension]
        surrogate_rows = solved[..., key_dimension:]
        query_key = jnp.where(
            causal_mask,
            jnp.einsum("hck,hdk->hcd", query_portion, key_part, precision=EXACT_PRECISION)
            * decay_ratio,
            0.0,
        )
        mixing_coefficient = query_portion * decay_factor_rows[:, :, None] - jnp.einsum(
            "hcd,hdk->hck", query_key, weight_matrix_rows, precision=EXACT_PRECISION
        )
        output_rows = jnp.einsum(
            "oum,omn->oun",
            mixing_coefficient,
            running_state[..., key_dimension:],
            precision=EXACT_PRECISION,
        )
        output_rows = output_rows + jnp.einsum(
            "hcd,hdv->hcv", query_key, surrogate_rows, precision=EXACT_PRECISION
        )
        state_coef = jnp.einsum(
            "hck,hkj->hcj",
            mixing_coefficient,
            running_state[..., :key_dimension],
            precision=EXACT_PRECISION,
        )
        trailing_keys = key_part * jnp.exp(cumulative[:, -1:] - cumulative)[:, :, None]
        weighted = jnp.einsum(
            "hck,hkz->hcz", weight_matrix_rows, running_state, precision=EXACT_PRECISION
        )
        updated_state = jnp.exp(cumulative[:, -1])[:, None, None] * running_state
        updated_state = updated_state - jnp.einsum(
            "hck,hcz->hkz", trailing_keys, weighted, precision=EXACT_PRECISION
        )
        update_term = jnp.einsum(
            "moe,mol->mel", trailing_keys, surrogate_rows, precision=EXACT_PRECISION
        )
        updated_state = updated_state + jnp.concatenate([square_zero, update_term], -1)
        return (updated_state, (output_rows, state_coef))

    inputs_all = (
        to_blocks(queries),
        to_blocks(key_rows),
        to_blocks(values),
        to_blocks(log_decay),
        to_blocks(beta_rows),
    )
    final_state, (block_outs, block_coefs) = lax.scan(advance, start_state, inputs_all)
    out_all = jnp.swapaxes(block_outs, 0, 1).reshape(head_count, row_count, value_size)
    coefficient_table = jnp.swapaxes(block_coefs, 0, 1).reshape(
        head_count, row_count, key_dimension
    )
    return (
        final_state[..., :key_dimension],
        final_state[..., key_dimension:],
        out_all,
        coefficient_table,
    )


def attention_output(local_output, coefficient_table, incoming_state, gate_in, head_norm):
    mixture_output = local_output + jnp.einsum(
        "oum,omn->oun", coefficient_table, incoming_state, precision=EXACT_PRECISION
    )
    head_count, row_count, value_size = mixture_output.shape
    gated = (
        mixture_output
        * lax.rsqrt(jnp.mean(mixture_output * mixture_output, axis=-1, keepdims=True) + EPSILON)
        * head_norm
    )
    gate_heads = jnp.swapaxes(gate_in.reshape(row_count, head_count, value_size), 0, 1)
    gated = gated * jax.nn.silu(gate_heads)
    return jnp.swapaxes(gated, 0, 1).reshape(row_count, head_count * value_size)


def on_device(
    hidden_in,
    out_grad,
    norm_attn,
    w_query,
    w_key,
    w_value,
    conv_query,
    conv_key,
    conv_value,
    w_alpha,
    w_beta,
    log_rate,
    rate_bias,
    w_gate_out,
    head_norm,
    w_out,
    norm_mlp,
    w_mlp_gate,
    w_mlp_up,
    w_mlp_down,
):
    bf16 = jnp.bfloat16
    f32 = jnp.float32
    slice_width = hidden_in.shape[1]
    offset = lax.axis_index("head") * slice_width
    head_count = log_rate.shape[0]
    key_width = w_query.shape[1]
    key_dimension = key_width // head_count
    value_size = w_value.shape[1] // head_count
    tap_count = conv_query.shape[0]
    edge_count = tap_count - 1

    def fetch_weights():
        return (
            lax.all_gather(w_query, "seq", axis=0, tiled=True),
            lax.all_gather(w_key, "seq", axis=0, tiled=True),
            lax.all_gather(w_value, "seq", axis=0, tiled=True),
            lax.all_gather(w_alpha, "seq", axis=0, tiled=True),
            lax.all_gather(w_beta, "seq", axis=0, tiled=True),
            lax.all_gather(w_gate_out, "seq", axis=0, tiled=True),
            lax.all_gather(w_out, "seq", axis=1, tiled=True),
            lax.all_gather(w_mlp_gate, "seq", axis=0, tiled=True),
            lax.all_gather(w_mlp_up, "seq", axis=0, tiled=True),
            lax.all_gather(w_mlp_down, "seq", axis=1, tiled=True),
        )

    full_in, full_grad = (
        lax.all_gather(hidden_in, "head", axis=1, tiled=True),
        lax.all_gather(out_grad, "head", axis=1, tiled=True),
    )
    (
        full_query,
        full_key,
        full_value,
        full_alpha,
        full_beta,
        full_gate_out,
        full_out,
        full_mlp_gate,
        full_mlp_up,
        full_mlp_down,
    ) = fetch_weights()
    normed_f, pull_one = jax.vjp(rms_gain, full_in.astype(f32), norm_attn)
    normed = normed_f.astype(bf16)
    projected = jnp.concatenate(
        [
            plain_dot(normed, full_query).astype(bf16),
            plain_dot(normed, full_key).astype(bf16),
            plain_dot(normed, full_value).astype(bf16),
        ],
        1,
    )
    alpha_in = plain_dot(normed, full_alpha)
    beta_in = plain_dot(normed, full_beta)
    gate_in = plain_dot(normed, full_gate_out)
    edge_rows = passed_along(projected[projected.shape[0] - edge_count :], "seq", 1)
    padded_rows = jnp.concatenate([edge_rows, projected], 0).astype(f32)
    conv_all = jnp.concatenate([conv_query, conv_key, conv_value], 1).astype(f32)
    mixer_fn = partial(mixer_inputs, key_dimension=key_dimension, value_size=value_size)
    (queries, key_rows, values, log_decay, beta_rows), pull_mix = jax.vjp(
        mixer_fn, padded_rows, conv_all, alpha_in, beta_in, log_rate, rate_bias
    )
    queries = queries.astype(bf16).astype(f32)
    key_rows = key_rows.astype(bf16).astype(f32)
    values = values.astype(bf16).astype(f32)
    (map_state, sum_state, local_output, coefficient_table), pull_block = jax.vjp(
        partial(block_states, length=BLOCK), queries, key_rows, values, log_decay, beta_rows
    )
    eye_block = jnp.broadcast_to(
        jnp.eye(key_dimension, dtype=f32), (head_count, key_dimension, key_dimension)
    )
    zero_state = jnp.zeros((head_count, key_dimension, value_size), f32)
    prior_map, incoming_state = prefix(
        (map_state, sum_state), "seq", combine_maps, (eye_block, zero_state)
    )
    attn_rows, pull_post = jax.vjp(
        attention_output, local_output, coefficient_table, incoming_state, gate_in, head_norm
    )
    attn_low = attn_rows.astype(bf16)
    attn_part = lax.psum_scatter(
        plain_dot(attn_low, full_out).astype(jnp.bfloat16), "head", scatter_dimension=1, tiled=True
    ).astype(jnp.float32)
    middle = (hidden_in.astype(f32) + attn_part).astype(bf16)
    full_middle = lax.all_gather(middle, "head", axis=1, tiled=True)
    normed_two_f, pull_two = jax.vjp(rms_gain, full_middle.astype(f32), norm_mlp)
    normed_two = normed_two_f.astype(bf16)
    gate_rows = plain_dot(normed_two, full_mlp_gate)
    up_rows = plain_dot(normed_two, full_mlp_up)
    sigmoid_gate = jax.nn.sigmoid(gate_rows)
    activated = gate_rows * sigmoid_gate
    inner = (activated * up_rows).astype(bf16)
    mlp_part = lax.psum_scatter(
        plain_dot(inner, full_mlp_down).astype(jnp.bfloat16),
        "head",
        scatter_dimension=1,
        tiled=True,
    ).astype(jnp.float32)
    output = (middle.astype(f32) + mlp_part).astype(bf16)
    (
        full_query,
        full_key,
        full_value,
        full_alpha,
        full_beta,
        full_gate_out,
        full_out,
        full_mlp_gate,
        full_mlp_up,
        full_mlp_down,
    ) = fetch_weights()
    d_inner = dot_last(full_grad, full_mlp_down)
    grad_down = dot_first(inner, full_grad)
    d_gate = (d_inner * up_rows * sigmoid_gate * (1.0 + gate_rows * (1.0 - sigmoid_gate))).astype(
        bf16
    )
    d_up = (d_inner * activated).astype(bf16)
    grad_gate = dot_first(normed_two, d_gate)
    grad_up = dot_first(normed_two, d_up)
    d_two = lax.psum(
        (dot_last(d_gate, full_mlp_gate) + dot_last(d_up, full_mlp_up)).astype(jnp.bfloat16), "head"
    ).astype(jnp.float32)
    d_full_middle, grad_norm_mlp = pull_two(d_two)
    d_middle = (
        out_grad.astype(f32) + lax.dynamic_slice_in_dim(d_full_middle, offset, slice_width, 1)
    ).astype(bf16)
    full_d_middle = lax.all_gather(d_middle, "head", axis=1, tiled=True)
    d_attn = dot_last(full_d_middle, full_out)
    grad_out_rows = dot_first(attn_low, full_d_middle)
    d_out_local, d_coef, d_state_local, d_gate_in, grad_head_norm = pull_post(d_attn)
    d_gate_low = d_gate_in.astype(bf16)
    later_map, state_output_gradient = prefix_2(
        (jnp.swapaxes(map_state, 1, 2), d_state_local), "seq", combine_maps, (eye_block, zero_state)
    )
    gradient_mapping = jnp.einsum(
        "bzm,bim->bzi", state_output_gradient, incoming_state, precision=EXACT_PRECISION
    )
    d_queries, d_keys, d_values, d_log_decay, d_beta = pull_block(
        (gradient_mapping, state_output_gradient, d_out_local, d_coef)
    )
    d_queries = d_queries.astype(bf16).astype(f32)
    d_keys = d_keys.astype(bf16).astype(f32)
    d_values = d_values.astype(bf16).astype(f32)
    d_padded, grad_conv_all, d_alpha, d_beta_in, grad_log_rate, grad_rate_bias = pull_mix(
        (d_queries, d_keys, d_values, d_log_decay, d_beta)
    )
    incoming = passed_along(d_padded[:edge_count], "seq", -1)
    d_own = d_padded[edge_count:]
    split_at = d_own.shape[0] - edge_count
    d_projected = jnp.concatenate([d_own[:split_at], d_own[split_at:] + incoming], 0).astype(bf16)
    d_q_raw = d_projected[:, :key_width]
    d_k_raw = d_projected[:, key_width : 2 * key_width]
    d_v_raw = d_projected[:, 2 * key_width :]
    d_alpha_low = d_alpha.astype(bf16)
    d_beta_low = d_beta_in.astype(bf16)
    grad_query_rows = dot_first(normed, d_q_raw)
    grad_key_rows = dot_first(normed, d_k_raw)
    grad_value_rows = dot_first(normed, d_v_raw)
    grad_alpha_rows = dot_first(normed, d_alpha_low)
    grad_beta_rows = dot_first(normed, d_beta_low)
    grad_gate_out_rows = dot_first(normed, d_gate_low)
    d_one_part = (
        dot_last(d_q_raw, full_query) + dot_last(d_k_raw, full_key) + dot_last(d_v_raw, full_value)
    )
    d_one_part = (
        d_one_part
        + dot_last(d_alpha_low, full_alpha)
        + dot_last(d_beta_low, full_beta)
        + dot_last(d_gate_low, full_gate_out)
    )
    d_one, grad_head_norm = (
        lax.psum(d_one_part.astype(jnp.bfloat16), "head").astype(jnp.float32),
        lax.psum(grad_head_norm.astype(jnp.bfloat16), "head").astype(jnp.float32),
    )
    d_full_in, grad_norm_attn = pull_one(d_one)
    grad_input = (
        d_middle.astype(f32) + lax.dynamic_slice_in_dim(d_full_in, offset, slice_width, 1)
    ).astype(bf16)
    (
        grad_query,
        grad_key,
        grad_value,
        grad_alpha,
        grad_beta,
        grad_gate_out,
        grad_out,
        grad_mlp_gate,
        grad_mlp_up,
        grad_mlp_down,
    ) = (
        lax.psum_scatter(
            grad_query_rows.astype(jnp.bfloat16), "seq", scatter_dimension=0, tiled=True
        ).astype(jnp.float32),
        lax.psum_scatter(
            grad_key_rows.astype(jnp.bfloat16), "seq", scatter_dimension=0, tiled=True
        ).astype(jnp.float32),
        lax.psum_scatter(
            grad_value_rows.astype(jnp.bfloat16), "seq", scatter_dimension=0, tiled=True
        ).astype(jnp.float32),
        lax.psum_scatter(
            grad_alpha_rows.astype(jnp.bfloat16), "seq", scatter_dimension=0, tiled=True
        ).astype(jnp.float32),
        lax.psum_scatter(
            grad_beta_rows.astype(jnp.bfloat16), "seq", scatter_dimension=0, tiled=True
        ).astype(jnp.float32),
        lax.psum_scatter(
            grad_gate_out_rows.astype(jnp.bfloat16), "seq", scatter_dimension=0, tiled=True
        ).astype(jnp.float32),
        lax.psum_scatter(
            grad_out_rows.astype(jnp.bfloat16), "seq", scatter_dimension=1, tiled=True
        ).astype(jnp.float32),
        lax.psum_scatter(
            grad_gate.astype(jnp.bfloat16), "seq", scatter_dimension=0, tiled=True
        ).astype(jnp.float32),
        lax.psum_scatter(
            grad_up.astype(jnp.bfloat16), "seq", scatter_dimension=0, tiled=True
        ).astype(jnp.float32),
        lax.psum_scatter(
            grad_down.astype(jnp.bfloat16), "seq", scatter_dimension=1, tiled=True
        ).astype(jnp.float32),
    )
    conv_q_part = grad_conv_all[:, :key_width]
    conv_k_part = grad_conv_all[:, key_width : 2 * key_width]
    conv_v_part = grad_conv_all[:, 2 * key_width :]
    (
        grad_conv_query,
        grad_conv_key,
        grad_conv_value,
        grad_log_rate,
        grad_rate_bias,
        grad_norm_attn,
        grad_norm_mlp,
        grad_head_norm,
    ) = (
        lax.psum(conv_q_part.astype(jnp.bfloat16), "seq").astype(jnp.float32),
        lax.psum(conv_k_part.astype(jnp.bfloat16), "seq").astype(jnp.float32),
        lax.psum(conv_v_part.astype(jnp.bfloat16), "seq").astype(jnp.float32),
        lax.psum(grad_log_rate.astype(jnp.bfloat16), "seq").astype(jnp.float32),
        lax.psum(grad_rate_bias.astype(jnp.bfloat16), "seq").astype(jnp.float32),
        lax.psum(grad_norm_attn.astype(jnp.bfloat16), "seq").astype(jnp.float32),
        lax.psum(grad_norm_mlp.astype(jnp.bfloat16), "seq").astype(jnp.float32),
        lax.psum(grad_head_norm.astype(jnp.bfloat16), "seq").astype(jnp.float32),
    )
    return (
        output,
        grad_input,
        grad_norm_attn,
        grad_query,
        grad_key,
        grad_value,
        grad_conv_query,
        grad_conv_key,
        grad_conv_value,
        grad_alpha,
        grad_beta,
        grad_log_rate,
        grad_rate_bias,
        grad_gate_out,
        grad_head_norm,
        grad_out,
        grad_norm_mlp,
        grad_mlp_gate,
        grad_mlp_up,
        grad_mlp_down,
    )


def solution(mesh):
    placed = (
        P("seq", "head"),
        P("seq", "head"),
        P(),
        P("seq", "head"),
        P("seq", "head"),
        P("seq", "head"),
        P(None, "head"),
        P(None, "head"),
        P(None, "head"),
        P("seq", "head"),
        P("seq", "head"),
        P("head"),
        P("head"),
        P("seq", "head"),
        P(),
        P("head", "seq"),
        P(),
        P("seq", "head"),
        P("seq", "head"),
        P("head", "seq"),
    )
    return jax.shard_map(
        on_device,
        mesh=mesh,
        in_specs=placed,
        out_specs=(
            P("seq", "head"),
            P("seq", "head"),
            P(),
            P("seq", "head"),
            P("seq", "head"),
            P("seq", "head"),
            P(None, "head"),
            P(None, "head"),
            P(None, "head"),
            P("seq", "head"),
            P("seq", "head"),
            P("head"),
            P("head"),
            P("seq", "head"),
            P(),
            P("head", "seq"),
            P(),
            P("seq", "head"),
            P("seq", "head"),
            P("head", "seq"),
        ),
        check_vma=False,
    )
```

profile of v0, /device:TPU:0, one launch (start us, length us, event | category | flops | bytes accessed | tf_op | source)
XLA Modules:
  0.0 2011.0 jit_solution(16524397334048172320)
XLA Ops:
  10.3 25.7 %all-gather.4 = bf16[32,64,4]{1,2,0:T(4,128)(2,1)S(1)} all-gather(bf16[1,64,4]{1,2,0:T(4,128)(2,1)} %bitcast.800), channel_id=1, replica_groups=mesh['seq'=32,'head'=4] {'seq'}, dimensions={0}, use_global_device_ids=true | all-gather | bytes 16896 | tf_op jit(solution)/shard_map/all_gather | solution.py:267
  36.2 23.6 %all-gather.5 = bf16[32,64,4]{1,2,0:T(4,128)(2,1)S(1)} all-gather(bf16[1,64,4]{1,2,0:T(4,128)(2,1)} %bitcast.801), channel_id=1, replica_groups=mesh['seq'=32,'head'=4] {'seq'}, dimensions={0}, use_global_device_ids=true | all-gather | bytes 16896 | tf_op jit(solution)/shard_map/all_gather | solution.py:268
  85.2 43.2 %all-gather.25.cloned.1.call-done = bf16[2048,512]{1,0:T(8,128)(2,1)} async-done(((bf16[64,512]{1,0:T(8,128)(2,1)}), bf16[2048,512]{1,0:T(8,128)(2,1)}) %all-gather.25.cloned.1.call-update) | async-done | bytes 2097168 | tf_op jit(solution)/shard_map/all_gather | solution.py:264
  130.7 45.4 %all-gather.29.cloned.1.call-done = bf16[2048,1024]{1,0:T(8,128)(2,1)} async-done(((bf16[64,1024]{1,0:T(8,128)(2,1)}), bf16[2048,1024]{1,0:T(8,128)(2,1)}) %all-gather.29.cloned.1.call-update) | async-done | bytes 4194320 | tf_op jit(solution)/shard_map/all_gather | solution.py:266
  211.8 186.4 %while.130 = (s32[]{:T(128)}, f32[4,128,384]{2,1,0:T(8,128)S(1)}, f32[4,4,64,256]{3,2,0,1:T(8,128)}, f32[4,4,64,128]{3,2,0,1:T(8,128)}, f32[4,4,64,64]{3,2,1,0:T...) while((s32[]{:T(128)}, f32[4,128,384]{2,1,0:T(8,128)S(1)}, ...), condition=%wide.region_5.6_spmd.clone.clone.clone, body=%wide.region_3.5_spmd.clone.clone.sunk.clone | while | flops 756585024 | bytes 19020632 | solution.py:201
  219.6 21.0 %custom-call.54 = f32[4,1,64,64]{2,3,1,0:T(8,128)} custom-call(f32[4,1,64,64]{3,2,1,0:T(8,128)} %add_bitcast_fusion.6), custom_call_target="InvertDiagBlocksLowerTriangular" | custom-call | tf_op jit(solution)/shard_map/jvp()/while/body/eval_jaxpr/triangular_solve | solution.py:151
  266.2 21.0 %custom-call.54 = f32[4,1,64,64]{2,3,1,0:T(8,128)} custom-call(f32[4,1,64,64]{3,2,1,0:T(8,128)} %add_bitcast_fusion.6), custom_call_target="InvertDiagBlocksLowerTriangular" | custom-call | tf_op jit(solution)/shard_map/jvp()/while/body/eval_jaxpr/triangular_solve | solution.py:151
  312.8 21.0 %custom-call.54 = f32[4,1,64,64]{2,3,1,0:T(8,128)} custom-call(f32[4,1,64,64]{3,2,1,0:T(8,128)} %add_bitcast_fusion.6), custom_call_target="InvertDiagBlocksLowerTriangular" | custom-call | tf_op jit(solution)/shard_map/jvp()/while/body/eval_jaxpr/triangular_solve | solution.py:151
  359.5 21.0 %custom-call.54 = f32[4,1,64,64]{2,3,1,0:T(8,128)} custom-call(f32[4,1,64,64]{3,2,1,0:T(8,128)} %add_bitcast_fusion.6), custom_call_target="InvertDiagBlocksLowerTriangular" | custom-call | tf_op jit(solution)/shard_map/jvp()/while/body/eval_jaxpr/triangular_solve | solution.py:151
  415.8 31.2 %all-gather.47.cloned.1.call-done = bf16[128,128,128]{2,1,0:T(8,128)(2,1)} async-done(((bf16[4,128,128]{2,1,0:T(8,128)(2,1)}), bf16[128,128,128]{2,1,0:T(8,128)(2,1)}) %all-gather.47.cloned.1.call-update) | async-done | bytes 4194320 | tf_op jit(solution)/shard_map/all_gather | solution.py:24
  447.0 55.0 %all-gather.49.cloned.1.call-done = bf16[128,128,256]{2,1,0:T(8,128)(2,1)} async-done(((bf16[4,128,256]{2,1,0:T(8,128)(2,1)}), bf16[128,128,256]{2,1,0:T(8,128)(2,1)}) %all-gather.49.cloned.1.call-update) | async-done | bytes 8388624 | tf_op jit(solution)/shard_map/all_gather | solution.py:24
  502.0 143.8 %while.132 = (s32[]{:T(128)}, f32[4,128,256]{2,1,0:T(8,128)}, s32[]{:T(128)}, bf16[32,4,128,128]{3,2,1,0:T(8,128)(2,1)}, bf16[32,4,128,256]{3,2,1,0:T(8,128)(2,1)}) while((s32[]{:T(128)}, f32[4,128,256]{2,1,0:T(8,128)}, s32[]{:T(128)}, bf16[32,4,128,128]{3,2,1,0:T(8,128)(2,1)}, ...), condition=%wide.region_7.8_spmd.clone.clone, body=%wide.region_6.7_spmd.clone.sunk.clone | while | flops 201981952 | bytes 3017303 | solution.py:37
  660.0 23.2 %reduce-scatter.17.cloned.1.call-done = bf16[256,512]{1,0:T(8,128)(2,1)} async-done(((bf16[256,2048]{1,0:T(8,128)(2,1)}), bf16[256,512]{1,0:T(8,128)(2,1)}) %reduce-scatter.17.cloned.1.call-update) | async-done | bytes 262160 | tf_op jit(solution)/shard_map/reduce_scatter | solution.py:329
  687.7 21.4 %all-gather.35.cloned.1.call-done = bf16[256,2048]{1,0:T(8,128)(2,1)} async-done(((bf16[256,512]{1,0:T(8,128)(2,1)}), bf16[256,2048]{1,0:T(8,128)(2,1)}) %all-gather.35.cloned.1.call-update) | async-done | bytes 1048592 | tf_op jit(solution)/shard_map/all_gather | solution.py:333
  710.6 49.8 %all-gather.37.cloned.1.call-done = bf16[2048,1376]{1,0:T(8,128)(2,1)} async-done(((bf16[64,1376]{1,0:T(8,128)(2,1)}), bf16[2048,1376]{1,0:T(8,128)(2,1)}) %all-gather.37.cloned.1.call-update) | async-done | bytes 5636112 | tf_op jit(solution)/shard_map/all_gather | solution.py:271
  767.0 43.3 %all-gather.39.cloned.1.call-done = bf16[2048,1376]{1,0:T(8,128)(2,1)} async-done(((bf16[64,1376]{1,0:T(8,128)(2,1)}), bf16[2048,1376]{1,0:T(8,128)(2,1)}) %all-gather.39.cloned.1.call-update) | async-done | bytes 5636112 | tf_op jit(solution)/shard_map/all_gather | solution.py:272
  835.0 51.2 %all-gather.41.cloned.1.call-done = bf16[1376,2048]{0,1:T(8,128)(2,1)} async-done(((bf16[1376,64]{0,1:T(8,128)(2,1)}), bf16[1376,2048]{0,1:T(8,128)(2,1)}) %all-gather.41.cloned.1.call-update) | async-done | bytes 5636112 | tf_op jit(solution)/shard_map/all_gather | solution.py:273
  904.8 41.6 %all-reduce.25.cloned.1.call-done = bf16[256,2048]{1,0:T(8,128)(2,1)} async-done(((bf16[256,2048]{1,0:T(8,128)(2,1)}), bf16[256,2048]{1,0:T(8,128)(2,1)}) %all-reduce.25.cloned.1.call-update) | async-done | bytes 1048592 | tf_op jit(solution)/shard_map/psum | solution.py:368
  954.0 22.5 %all-gather.45.cloned.1.call-done = bf16[256,2048]{1,0:T(8,128)(2,1)} async-done(((bf16[256,512]{1,0:T(8,128)(2,1)}), bf16[256,2048]{1,0:T(8,128)(2,1)}) %all-gather.45.cloned.1.call-update) | async-done | bytes 1048592 | tf_op jit(solution)/shard_map/all_gather | solution.py:375
  1032.7 48.3 %all-gather.53.cloned.1.call-done = bf16[128,128,256]{2,1,0:T(8,128)(2,1)} async-done(((bf16[4,128,256]{2,1,0:T(8,128)(2,1)}), bf16[128,128,256]{2,1,0:T(8,128)(2,1)}) %all-gather.53.cloned.1.call-update) | async-done | bytes 8388624 | tf_op jit(solution)/shard_map/all_gather | solution.py:43
  1081.0 107.9 %while.133 = (s32[]{:T(128)}, f32[4,128,256]{2,1,0:T(8,128)}, s32[]{:T(128)}, bf16[32,4,128,128]{3,2,1,0:T(8,128)(2,1)}, bf16[32,4,128,256]{3,2,1,0:T(8,128)(2,1)}) while((s32[]{:T(128)}, f32[4,128,256]{2,1,0:T(8,128)}, s32[]{:T(128)}, bf16[32,4,128,128]{3,2,1,0:T(8,128)(2,1)}, ...), condition=%wide.region_16.17_spmd.clone.clone, body=%wide.region_15.16_spmd.clone.sunk.clone | while | flops 201981952 | bytes 3017349 | solution.py:59
  1193.0 231.9 %while.131 = (s32[]{:T(128)}, f32[4,128,384]{2,1,0:T(8,128)S(1)}, bf16[4,4,64,128]{3,2,0,1:T(8,128)(2,1)}, bf16[4,4,64,128]{3,2,0,1:T(8,128)(2,1)}, bf16[4,4,64,...) while((s32[]{:T(128)}, f32[4,128,384]{2,1,0:T(8,128)S(1)}, ...), condition=%wide.region_28.29_spmd.clone.clone.clone, body=%wide.region_17.28_spmd.clone.clone.sunk.clone | while | flops 1525724416 | bytes 49285888 | solution.py:201
  1210.5 21.0 %custom-call.55 = f32[4,1,64,64]{2,3,1,0:T(8,128)} custom-call(f32[4,1,64,64]{3,2,1,0:T(8,128)} %add_bitcast_fusion.7), custom_call_target="InvertDiagBlocksLowerTriangular" | custom-call | tf_op jit(solution)/shard_map/transpose(jvp())/while/body/eval_jaxpr/triangular_solve | solution.py:151
  1326.2 21.0 %custom-call.55 = f32[4,1,64,64]{2,3,1,0:T(8,128)} custom-call(f32[4,1,64,64]{3,2,1,0:T(8,128)} %add_bitcast_fusion.7), custom_call_target="InvertDiagBlocksLowerTriangular" | custom-call | tf_op jit(solution)/shard_map/transpose(jvp())/while/body/eval_jaxpr/triangular_solve | solution.py:151
  1384.0 21.0 %custom-call.55 = f32[4,1,64,64]{2,3,1,0:T(8,128)} custom-call(f32[4,1,64,64]{3,2,1,0:T(8,128)} %add_bitcast_fusion.7), custom_call_target="InvertDiagBlocksLowerTriangular" | custom-call | tf_op jit(solution)/shard_map/transpose(jvp())/while/body/eval_jaxpr/triangular_solve | solution.py:151
  1492.9 51.4 %reduce-scatter.29.cloned.1.call-done = bf16[1024,64]{0,1:T(8,128)(2,1)} async-done(((bf16[1024,2048]{0,1:T(8,128)(2,1)}), bf16[1024,64]{0,1:T(8,128)(2,1)}) %reduce-scatter.29.cloned.1.call-update) | async-done | bytes 131088 | tf_op jit(solution)/shard_map/reduce_scatter | solution.py:457
  1546.0 78.2 %reduce-scatter.37.cloned.1.call-done = bf16[64,4]{1,0:T(8,128)(2,1)} async-done(((bf16[2048,4]{1,0:T(8,128)(2,1)}), bf16[64,4]{1,0:T(8,128)(2,1)}) %reduce-scatter.37.cloned.1.call-update) | async-done | bytes 528
  1625.6 78.3 %reduce-scatter.39.cloned.1.call-done = bf16[64,4]{1,0:T(8,128)(2,1)} async-done(((bf16[2048,4]{1,0:T(8,128)(2,1)}), bf16[64,4]{1,0:T(8,128)(2,1)}) %reduce-scatter.39.cloned.1.call-update) | async-done | bytes 528
  1705.3 45.8 %all-reduce.27.cloned.1.call-done = bf16[256,2048]{1,0:T(8,128)(2,1)} async-done(((bf16[256,2048]{1,0:T(8,128)(2,1)}), bf16[256,2048]{1,0:T(8,128)(2,1)}) %all-reduce.27.cloned.1.call-update) | async-done | bytes 1048592 | tf_op jit(solution)/shard_map/psum | solution.py:420
  1754.4 127.2 %all-reduce.21 = (bf16[2048]{0:T(1024)(128)(2,1)S(1)}, bf16[4,512]{1,0:T(4,128)(2,1)S(1)}, bf16[4,512]{1,0:T(4,128)(2,1)S(1)}, bf16[4,1024]{1,0:T(4,128)(2,1)S(1...) all-reduce(bf16[2048]{0:T(1024)(128)(2,1)S(1)} %get-tuple-element.2, ...), channel_id=1, replica_groups=mesh['seq'=32,'head'=4] {'seq'}, use_global_device_ids=true, to_apply=%region_34.35 | all-reduce | flops 12552 | bytes 50208 | tf_op jit(solution)/shard_map/psum | solution.py:488
  1889.9 27.2 %reduce-scatter.23.cloned.1.call-done = bf16[64,512]{1,0:T(8,128)(2,1)} async-done(((bf16[2048,512]{1,0:T(8,128)(2,1)}), bf16[64,512]{1,0:T(8,128)(2,1)}) %reduce-scatter.23.cloned.1.call-update) | async-done | bytes 65552 | tf_op jit(solution)/shard_map/reduce_scatter | solution.py:442
  1918.6 83.8 %reduce-scatter.25.cloned.1.call-done = bf16[64,1024]{1,0:T(8,128)(2,1)} async-done(((bf16[2048,1024]{1,0:T(8,128)(2,1)}), bf16[64,1024]{1,0:T(8,128)(2,1)}) %reduce-scatter.25.cloned.1.call-update) | async-done | bytes 131088 | tf_op jit(solution)/shard_map/reduce_scatter | solution.py:445
  (1063 shorter events, 828.2 us)
Async XLA Ops:
  7.3 53.5 %all-gather.23.cloned.1.call-start = ((), (), s32[]{:S(2)}) async-start(), calls=%async_computation.12 | async-start | bytes 1310720 | tf_op jit(solution)/shard_map/all_gather | solution.py:277
  8.0 74.8 %all-gather.27.cloned.1.call-start = ((), (), s32[]{:S(2)}) async-start(), calls=%async_computation.14 | async-start | bytes 2162688 | tf_op jit(solution)/shard_map/all_gather | solution.py:265
  8.7 119.6 %all-gather.25.cloned.1.call-start = ((), (), s32[]{:S(2)}) async-start(), calls=%async_computation.13 | async-start | bytes 2162688 | tf_op jit(solution)/shard_map/all_gather | solution.py:264
  9.5 166.7 %all-gather.29.cloned.1.call-start = ((), (), s32[]{:S(2)}) async-start(), calls=%async_computation.15 | async-start | bytes 4325376 | tf_op jit(solution)/shard_map/all_gather | solution.py:266
  10.0 436.9 %all-gather.47.cloned.1.call-start = ((), (), s32[]{:S(2)}) async-start(), calls=%async_computation.36 | async-start | bytes 4325376 | tf_op jit(solution)/shard_map/all_gather | solution.py:24
  179.7 3.8 collective-permute-start
  398.9 103.1 %all-gather.49.cloned.1.call-start = ((), (), s32[]{:S(2)}) async-start(), calls=%async_computation.37 | async-start | bytes 8650752 | tf_op jit(solution)/shard_map/all_gather | solution.py:24
  399.7 249.8 %all-gather.31.cloned.1.call-start = ((), (), s32[]{:S(2)}) async-start(), calls=%async_computation.16 | async-start | bytes 4325376 | tf_op jit(solution)/shard_map/all_gather | solution.py:269
  400.4 254.8 %all-gather.33.cloned.1.call-start = ((), (), s32[]{:S(2)}) async-start(), calls=%async_computation.17 | async-start | bytes 4325376 | tf_op jit(solution)/shard_map/all_gather | solution.py:270
  401.2 282.0 %reduce-scatter.17.cloned.1.call-start = ((), (), s32[]{:S(2)}) async-start(), calls=%async_computation.18 | async-start | bytes 1310720 | tf_op jit(solution)/shard_map/reduce_scatter | solution.py:329
  660.0 49.1 %all-gather.35.cloned.1.call-start = ((), (), s32[]{:S(2)}) async-start(), calls=%async_computation.19 | async-start | bytes 1310720 | tf_op jit(solution)/shard_map/all_gather | solution.py:333
  685.0 75.4 %all-gather.37.cloned.1.call-start = ((), (), s32[]{:S(2)}) async-start(), calls=%async_computation.20 | async-start | bytes 5947392 | tf_op jit(solution)/shard_map/all_gather | solution.py:271
  685.8 124.5 %all-gather.39.cloned.1.call-start = ((), (), s32[]{:S(2)}) async-start(), calls=%async_computation.21 | async-start | bytes 5947392 | tf_op jit(solution)/shard_map/all_gather | solution.py:272
  686.3 148.6 %all-gather.43.cloned.1.call-start = ((), (), s32[]{:S(2)}) async-start(), calls=%async_computation.24 | async-start | bytes 1310720 | tf_op jit(solution)/shard_map/all_gather | solution.py:278
  687.1 199.1 %all-gather.41.cloned.1.call-start = ((), (), s32[]{:S(2)}) async-start(), calls=%async_computation.22 | async-start | bytes 5947392 | tf_op jit(solution)/shard_map/all_gather | solution.py:273
  687.7 258.7 %all-reduce.25.cloned.1.call-start = ((), (), s32[]{:S(2)}) async-start(), calls=%async_computation.25 | async-start | bytes 2097152 | tf_op jit(solution)/shard_map/psum | solution.py:368
  901.5 75.0 %all-gather.45.cloned.1.call-start = ((), (), s32[]{:S(2)}) async-start(), calls=%async_computation.26 | async-start | bytes 1310720 | tf_op jit(solution)/shard_map/all_gather | solution.py:375
  951.5 81.1 %all-gather.51.cloned.1.call-start = ((), (), s32[]{:S(2)}) async-start(), calls=%async_computation.38 | async-start | bytes 4325376 | tf_op jit(solution)/shard_map/all_gather | solution.py:43
  954.0 127.0 %all-gather.53.cloned.1.call-start = ((), (), s32[]{:S(2)}) async-start(), calls=%async_computation.39 | async-start | bytes 8650752 | tf_op jit(solution)/shard_map/all_gather | solution.py:43
  986.0 488.0 %reduce-scatter.19.cloned.1.call-start = ((), (), s32[]{:S(2)}) async-start(), calls=%async_computation.23 | async-start | bytes 1310720 | tf_op jit(solution)/shard_map/reduce_scatter | solution.py:341
  991.8 494.4 %reduce-scatter.31.cloned.1.call-start = ((), (), s32[]{:S(2)}) async-start(), calls=%async_computation.33 | async-start | bytes 5947392 | tf_op jit(solution)/shard_map/reduce_scatter | solution.py:460
  997.8 490.2 %reduce-scatter.33.cloned.1.call-start = ((), (), s32[]{:S(2)}) async-start(), calls=%async_computation.34 | async-start | bytes 5947392 | tf_op jit(solution)/shard_map/reduce_scatter | solution.py:463
  1003.6 486.0 %reduce-scatter.35.cloned.1.call-start = ((), (), s32[]{:S(2)}) async-start(), calls=%async_computation.35 | async-start | bytes 5947392 | tf_op jit(solution)/shard_map/reduce_scatter | solution.py:466
  1009.6 481.7 %reduce-scatter.27.cloned.1.call-start = ((), (), s32[]{:S(2)}) async-start(), calls=%async_computation.31 | async-start | bytes 4325376 | tf_op jit(solution)/shard_map/reduce_scatter | solution.py:454
  1014.3 530.0 %reduce-scatter.29.cloned.1.call-start = ((), (), s32[]{:S(2)}) async-start(), calls=%async_computation.32 | async-start | bytes 4325376 | tf_op jit(solution)/shard_map/reduce_scatter | solution.py:457
  1026.8 597.3 %reduce-scatter.37.cloned.1.call-start = ((), (), s32[]{:S(2)}) async-start(), calls=%async_computation.40 | async-start | bytes 540672
  1443.0 11.7 collective-permute-start.1
  1451.9 252.0 %reduce-scatter.39.cloned.1.call-start = ((), (), s32[]{:S(2)}) async-start(), calls=%async_computation.41 | async-start | bytes 540672
  1454.6 296.5 %all-reduce.27.cloned.1.call-start = ((), (), s32[]{:S(2)}) async-start(), calls=%async_computation.27 | async-start | bytes 2097152 | tf_op jit(solution)/shard_map/psum | solution.py:420
  1464.2 424.2 %reduce-scatter.21.cloned.1.call-start = ((), (), s32[]{:S(2)}) async-start(), calls=%async_computation.28 | async-start | bytes 2162688 | tf_op jit(solution)/shard_map/reduce_scatter | solution.py:439
  1466.4 450.6 %reduce-scatter.23.cloned.1.call-start = ((), (), s32[]{:S(2)}) async-start(), calls=%async_computation.29 | async-start | bytes 2162688 | tf_op jit(solution)/shard_map/reduce_scatter | solution.py:442
  1468.9 533.5 %reduce-scatter.25.cloned.1.call-start = ((), (), s32[]{:S(2)}) async-start(), calls=%async_computation.30 | async-start | bytes 4325376 | tf_op jit(solution)/shard_map/reduce_scatter | solution.py:445
  (188 other events, 3173.7 us)
Sparse Core Ops, SparseCore 0:
  9.8 26.3 all-gather.22
  38.4 44.3 all-gather.26
  85.1 43.2 all-gather.24
  130.5 45.6 all-gather.28
  399.0 47.9 all-gather.46
  449.7 52.2 all-gather.48
  504.3 45.9 all-gather.30
  552.5 45.6 all-gather.32
  660.1 23.0 reduce-scatter.16
  685.4 23.6 all-gather.34
  711.6 48.7 all-gather.36
  762.8 47.4 all-gather.38
  812.0 22.9 all-gather.42
  837.3 48.7 all-gather.40
  901.6 44.6 all-reduce.24
  951.7 24.7 all-gather.44
  979.2 46.7 all-gather.50
  1028.7 52.2 all-gather.52
  1083.4 22.9 reduce-scatter.18
  1110.5 85.1 reduce-scatter.30
  1199.5 84.9 reduce-scatter.32
  1288.7 84.9 reduce-scatter.34
  1377.4 81.6 reduce-scatter.26
  1463.0 81.2 reduce-scatter.28
  1547.8 76.3 reduce-scatter.36
  1627.5 76.3 reduce-scatter.38
  1706.1 44.9 all-reduce.26
  1755.0 79.8 reduce-scatter.20
  1838.8 78.1 reduce-scatter.22
  1921.0 81.3 reduce-scatter.24
where the time goes:
time: 2020 us; the launch traced here: 2010 us
  waiting for transfers between devices  884 us (44%)
  matrix products  426 us (21%)
  other arithmetic  280 us (14%)
  local copies, waits for them, and re-layouts  197 us (10%)
  blocking collectives  187 us (9%)
    another operation x40, other arithmetic, advance(): lax.linalg.triangular_solve(system, right_side, left_side=True, lower=Tru...  178 us
    unnamed x32, waiting for transfers between devices  163 us
    dot_general x64, matrix products, combine_maps(): jnp.einsum('hij,hjk->hik', later[0], earlier[1], precision=EXACT_PRECISION)  158 us
    psum x1, blocking collectives, on_device(): lax.psum(grad_norm_attn.astype(jnp.bfloat16), 'seq').astype(jnp.float32)  127 us
    while x280, local copies, waits for them, and re-layouts  101 us
    all_gather x2, waiting for transfers between devices, prefix(): lax.all_gather(part.astype(kind), axis)  86.2 us
    reduce_scatter x1, waiting for transfers between devices, on_device(): lax.psum_scatter(grad_value_rows.astype(jnp.bfloat16), 'seq', scatter_dim...  83.8 us
    reduce_scatter x1, waiting for transfers between devices, on_device(): lax.psum_scatter(grad_out_rows.astype(jnp.bfloat16), 'seq', scatter_dimen...  51.4 us
  transfers between devices with their start and end apart: 32, of which 20 were waited for; matrix products, arithmetic and copies ran while one was open for 32% of the time, Pallas kernels for 0%

commit v1 on v0

v1 whole, which is shorter than its diff:
```python
from functools import partial

import jax
import jax.numpy as jnp
from jax import lax
from jax.experimental import pallas as pl
from jax.experimental.pallas import tpu as pltpu
from jax.sharding import PartitionSpec as P

EPSILON = 1e-06
F32 = jnp.float32
BF16 = jnp.bfloat16
C = 128
DK = 128
DV = 256
H = 2
TAPS = 4
VMEM = 56 * 1024 * 1024
NZ, NY, NC = 4, 4, 2
NX = 4
PAIR = 2
ROWS = PAIR * C


def mm(a, b):
    return jnp.dot(a.astype(BF16), b.astype(BF16), preferred_element_type=F32)


def nt(a, b):
    return lax.dot_general(
        a.astype(BF16), b.astype(BF16), (((1,), (1,)), ((), ())), preferred_element_type=F32
    )


def tn(a, b):
    return lax.dot_general(
        a.astype(BF16), b.astype(BF16), (((0,), (0,)), ((), ())), preferred_element_type=F32
    )


def halves(b):
    hi = b.astype(BF16)
    return hi, (b - hi.astype(F32)).astype(BF16)


def mm_two(a, b):
    hi, lo = halves(b)
    return mm(a, hi) + mm(a, lo)


def tn_two(a, b):
    hi, lo = halves(b)
    return tn(a, hi) + tn(a, lo)


def mm_three(a, b):
    a_hi, a_lo = halves(a)
    b_hi, b_lo = halves(b)
    return mm(a_hi, b_hi) + (mm(a_hi, b_lo) + mm(a_lo, b_hi))


def mm_ones(ones, b):
    hi, rest = halves(b)
    low = (b - hi.astype(F32)) - rest.astype(F32)
    return mm(ones, hi) + (mm(ones, rest) + mm(ones, low))


def iotas(rows, columns):
    return (
        lax.broadcasted_iota(jnp.int32, (rows, columns), 0),
        lax.broadcasted_iota(jnp.int32, (rows, columns), 1),
    )


def unit_lower_inverse(lows):
    row, col = iotas(C, C)
    eye = (row == col).astype(F32)
    same = (row >> 3) == (col >> 3)
    base = [jnp.where(same, n, 0.0) for n in lows]
    square = [mm(b, b) for b in base]
    cross = [mm(b, s) for b, s in zip(base, square)]
    fourth = [mm(s, s) for s in square]
    partial_inv = [eye - b + s - c for b, s, c in zip(base, square, cross)]
    extra = [mm(p, f) for p, f in zip(partial_inv, fourth)]
    inverse = [p + e for p, e in zip(partial_inv, extra)]
    level = 3
    while (1 << level) < C:
        pair = ((row >> (level + 1)) == (col >> (level + 1))) & ((row >> level) != (col >> level))
        off = [jnp.where(pair, n, 0.0) for n in lows]
        right = [mm(o, t) for o, t in zip(off, inverse)]
        step = [mm(t, r) for t, r in zip(inverse, right)]
        inverse = [t - s for t, s in zip(inverse, step)]
        level += 1
    residual = [eye - t - mm_three(n, t) for n, t in zip(lows, inverse)]
    fix = [mm(t, r) for t, r in zip(inverse, residual)]
    return [t + f for t, f in zip(inverse, fix)]


def conv_apply(window, taps):
    count = window.shape[0] - 16
    out = window[13 : 13 + count] * taps[0:1]
    for j in range(1, TAPS):
        out = out + window[13 + j : 13 + j + count] * taps[j : j + 1]
    return out


def conv_window(before, current):
    return jnp.concatenate([before, current], 0).astype(BF16).astype(F32)


def softplus(v):
    return jnp.maximum(v, 0.0) + jnp.log1p(jnp.exp(-jnp.abs(v)))


def gates_of(ab, rates):
    row, col = iotas(C, C)
    log_decay = rates[0:1] * softplus(ab + rates[1:2])
    cumulative = mm_ones((row >= col).astype(F32), log_decay)
    return jnp.where(col < H, cumulative, jax.nn.sigmoid(ab))


def decay_ratio(column, line):
    row, col = iotas(C, C)
    return jnp.exp(jnp.where(row >= col, column - line, 0.0))


def block(j):
    return slice(j * C, (j + 1) * C)


def head_keys(h):
    return slice(h * DK, (h + 1) * DK)


def head_values(h):
    return slice(h * DV, (h + 1) * DV)


CHAINS = [(j, h) for j in range(PAIR) for h in range(H)]


def chunk_forward_kernel(
    where_ref, x_ref, before_ref, edge_ref, ab_ref, taps_ref, rates_ref,
    q_ref, k_ref, v_ref, gates_ref, p_ref, t_ref, w_ref, u_ref, map_ref, state,
):
    n = pl.program_id(0)
    row, col = iotas(C, C)
    before = jnp.where(n == 0, edge_ref[...], before_ref[...])
    window = conv_window(before, x_ref[...])
    conv = conv_apply(window, taps_ref[...])
    act = conv * jax.nn.sigmoid(conv)
    all_gates = [gates_of(ab_ref[block(j)], rates_ref[...]) for j in range(PAIR)]
    lines = [a.T for a in all_gates]
    for j in range(PAIR):
        gates_ref[block(j)] = all_gates[j]
    qs, ks, vs = [], [], []
    for h in range(H):
        q = act[:, head_keys(h)]
        k = act[:, head_keys(H + h)]
        q = q * lax.rsqrt(jnp.sum(q * q, -1, keepdims=True) + EPSILON) * DK ** (-0.5)
        k = k * lax.rsqrt(jnp.sum(k * k, -1, keepdims=True) + EPSILON)
        qs.append(q.astype(BF16))
        ks.append(k.astype(BF16))
        vs.append(act[:, 2 * H * DK + h * DV : 2 * H * DK + (h + 1) * DV].astype(BF16))
        q_ref[:, head_keys(h)] = qs[h]
        k_ref[:, head_keys(h)] = ks[h]
        v_ref[:, head_values(h)] = vs[h]
    q = [qs[h][block(j)] for j, h in CHAINS]
    k = [ks[h][block(j)] for j, h in CHAINS]
    v = [vs[h][block(j)] for j, h in CHAINS]
    g = [all_gates[j][:, h : h + 1] for j, h in CHAINS]
    beta = [all_gates[j][:, H + h : H + h + 1] for j, h in CHAINS]
    ratio = [decay_ratio(g[c], lines[j][h : h + 1]) for c, (j, h) in enumerate(CHAINS)]
    chains = range(len(CHAINS))
    gram = [nt(k[c], k[c]) for c in chains]
    score = [nt(q[c], k[c]) for c in chains]
    low = [beta[c] * jnp.where(row > col, gram[c] * ratio[c], 0.0) for c in chains]
    inverse = [t.astype(BF16) for t in unit_lower_inverse(low)]
    growth = [jnp.exp(g[c]) for c in chains]
    wide_k = [k[c].astype(F32) * (beta[c] * growth[c]) for c in chains]
    wide_v = [v[c].astype(F32) * beta[c] for c in chains]
    w = [mm(inverse[c], wide_k[c]).astype(BF16) for c in chains]
    u = [mm(inverse[c], wide_v[c]) for c in chains]
    for c, (j, h) in enumerate(CHAINS):
        p_ref[j, h] = jnp.where(row >= col, score[c] * ratio[c], 0.0).astype(BF16)
        t_ref[j, h] = inverse[c]
        w_ref[j, h] = w[c]
        u_ref[j, h] = u[c]

    @pl.when(n == 0)
    def _():
        for h in range(H):
            state[h] = jnp.concatenate(
                [(row == col).astype(F32), jnp.zeros((DK, DV), F32)], 1
            )

    for c, (j, h) in enumerate(CHAINS):
        old = state[h]
        total = g[c][C - 1 : C]
        trail = k[c].astype(F32) * jnp.exp(total - g[c])
        delta = jnp.concatenate([jnp.zeros((C, DK), F32), u[c]], 1) - mm(w[c], old)
        state[h] = jnp.exp(total) * old + tn(trail, delta)

    @pl.when(n == pl.num_programs(0) - 1)
    def _():
        map_ref[...] = state[...].astype(BF16)


def ring_parts(refs):
    own, one, top, bottom, three = refs
    return [
        [own.at[0], own.at[1]], [one.at[0], one.at[1]],
        [top.at[0], bottom.at[0]], [three.at[0], three.at[1]],
    ]


def line_map_kernel(place_ref, *refs):
    y = place_ref[0]
    parts, (out_ref, held) = ring_parts(refs[:5]), refs[5:]
    for k in range(NY):
        for h in range(H):
            held[k, h] = parts[k][h][...]
    totals = [held[y, h].astype(F32) for h in range(H)]
    for j in range(1, NY):
        k = lax.rem(y - j + NY, NY)
        for h in range(H):
            new = held[k, h]
            totals[h] = mm_two(new[:, :DK], totals[h]) + jnp.concatenate(
                [jnp.zeros((DK, DK), F32), new[:, DK:].astype(F32)], 1
            )
    for h in range(H):
        out_ref[h] = totals[h].astype(BF16)


def chunk_output_kernel(where_ref, *refs):
    along, across, refs = ring_parts(refs[:5]), ring_parts(refs[5:10]), refs[10:]
    (q_ref, k_ref, gates_ref, p_ref, w_ref, u_ref, gate_ref, gain_ref,
     mixed_ref, attn_ref, d_ref, s_ref, state) = refs
    n = pl.program_id(0)
    y, z = where_ref[1], where_ref[2]

    @pl.when(n == 0)
    def _():
        s = [jnp.zeros((DK, DV), F32) for _ in range(H)]
        for place, maps in ((z, across), (y, along)):
            for shift in (3, 2, 1):
                for h in range(H):
                    m = maps[shift][h]
                    new = mm_two(m[:, :DK], s[h]) + m[:, DK:].astype(F32)
                    s[h] = jnp.where(place >= shift, new, s[h])
        for h in range(H):
            state[h] = s[h]

    gain = gain_ref[...]
    for j, h in CHAINS:
        g = gates_ref[block(j), h : h + 1]
        total = g[C - 1 : C]
        s = state[h]
        held = s.astype(BF16)
        s_ref[j, h] = held
        q = q_ref[block(j), head_keys(h)].astype(F32) * jnp.exp(g)
        delta = (u_ref[j, h] - mm(w_ref[j, h], held)).astype(BF16)
        d_ref[j, h] = delta
        out = mm(q, held) + mm(p_ref[j, h], delta)
        trail = k_ref[block(j), head_keys(h)].astype(F32) * jnp.exp(total - g)
        state[h] = jnp.exp(total) * s + tn(trail, delta)
        mixed_ref[block(j), head_values(h)] = out
        gate = gate_ref[block(j), head_values(h)]
        r = lax.rsqrt(jnp.mean(out * out, -1, keepdims=True) + EPSILON)
        attn = out * r * gain * (gate * jax.nn.sigmoid(gate))
        attn_ref[block(j), head_values(h)] = attn.astype(BF16)


def chunk_adjoint_kernel(
    where_ref, own_ref, other_ref, wa_ref, mixed_ref, gate_ref, gain_ref, q_ref, k_ref,
    gates_ref, p_ref, w_ref,
    dm_ref, dg_ref, gain_out_ref, pd_ref, qd_ref, n_ref, state,
):
    i = pl.program_id(0)
    last = pl.num_programs(0) - 1

    @pl.when(i == 0)
    def _():
        state[...] = jnp.zeros_like(state)
        gain_out_ref[...] = jnp.zeros_like(gain_out_ref)

    mine = (last - i) == where_ref[0]
    d_attn = mm(jnp.where(mine, own_ref[...], other_ref[...]), wa_ref[...])
    gain = gain_ref[...]
    for j, h in reversed(CHAINS):
        rows, cols = block(j), head_values(h)
        da, mixed, gate = d_attn[rows, cols], mixed_ref[rows, cols], gate_ref[rows, cols]
        r = lax.rsqrt(jnp.mean(mixed * mixed, -1, keepdims=True) + EPSILON)
        m = mixed * r
        s = jax.nn.sigmoid(gate)
        z = gate * s
        e = da * gain * z
        dm = (r * (e - m * jnp.mean(e * m, -1, keepdims=True))).astype(BF16)
        dm_ref[rows, cols] = dm
        dg_ref[rows, cols] = (da * gain * m * (s * (1.0 + gate * (1.0 - s)))).astype(BF16)
        gain_out_ref[0:1] += jnp.sum(da * m * z, 0, keepdims=True)
        g = gates_ref[rows, h : h + 1]
        total = g[C - 1 : C]
        q = q_ref[rows, head_keys(h)].astype(F32) * jnp.exp(g)
        trail = k_ref[rows, head_keys(h)].astype(F32) * jnp.exp(total - g)
        p_dm, q_dm = tn(p_ref[j, h], dm), tn(q, dm)
        pd_ref[j, h], qd_ref[j, h] = p_dm, q_dm
        old = state[h]
        state[h] = jnp.exp(total) * old + q_dm - tn(w_ref[j, h], p_dm + mm(trail, old))

    @pl.when(i == last)
    def _():
        n_ref[...] = state[...].astype(BF16)


def line_adjoint_kernel(place_ref, *refs):
    y = place_ref[0]
    parts, rest = ring_parts(refs[:5]), refs[5:]
    ins, (out_ref, maps, held) = rest[:NY], rest[NY:]
    for k in range(NY):
        held[k] = ins[k][...]
        for h in range(H):
            maps[k, h] = parts[k][h][:, :DK]
    last = lax.rem(y + 1, NY)
    totals = [held[last, h].astype(F32) for h in range(H)]
    for j in range(NY - 2, -1, -1):
        k = lax.rem(y - j + NY, NY)
        for h in range(H):
            totals[h] = tn_two(maps[k, h], totals[h]) + held[k, h].astype(F32)
    for h in range(H):
        out_ref[h] = totals[h].astype(BF16)


def conv_backward(n, i, d_act, window, taps, carry, dx_ref, tail_ref, front_ref, taps_out_ref):
    conv = conv_apply(window, taps)
    s = jax.nn.sigmoid(conv)
    grad = d_act(conv * s) * (s * (1.0 + conv * (1.0 - s)))
    count, wide = grad.shape
    for j in range(TAPS):
        taps_out_ref[j : j + 1] += jnp.sum(
            grad * window[13 + j : 13 + j + count], 0, keepdims=True
        )
    longer = jnp.concatenate([grad, carry[...]], 0)
    d_x = longer[0:count] * taps[TAPS - 1 : TAPS]
    for j in range(TAPS - 1):
        d_x = d_x + longer[TAPS - 1 - j : TAPS - 1 - j + count] * taps[j : j + 1]
    dx_ref[:, :wide] = d_x.astype(BF16)
    carry[...] = grad[0:8]

    @pl.when(i == 0)
    def _():
        tail_ref[...] = d_x[count - 16 :]

    @pl.when(n == 0)
    def _():
        first = jnp.concatenate([jnp.zeros((16, wide), F32), grad[0:8]], 0)
        front = jnp.zeros((16, wide), F32)
        for j in range(TAPS - 1):
            front = front + first[TAPS - 1 - j : TAPS - 1 - j + 16] * taps[j : j + 1]
        front_ref[...] = front


def stacked(pieces, h):
    found = [piece for piece, (_, head) in zip(pieces, CHAINS) if head == h]
    return jnp.concatenate([piece.astype(BF16).astype(F32) for piece in found], 0)


def unit_back(raw, f):
    r = lax.rsqrt(jnp.sum(raw * raw, -1, keepdims=True) + EPSILON)
    unit = raw * r
    return (f - unit * jnp.sum(unit * f, -1, keepdims=True)) * r


def chunk_query_kernel(
    where_ref, x_ref, before_ref, edge_ref, taps_ref, q_ref, k_ref, gates_ref, p_ref, d_ref,
    s_ref, dm_ref,
    dx_ref, tail_ref, front_ref, taps_out_ref, dk_ref, dg_ref, carry,
):
    i = pl.program_id(0)
    n = pl.num_programs(0) - 1 - i
    row, col = iotas(C, C)
    chains = range(len(CHAINS))

    @pl.when(i == 0)
    def _():
        carry[...] = jnp.zeros_like(carry)
        taps_out_ref[...] = jnp.zeros_like(taps_out_ref)

    all_gates = [gates_ref[block(j)] for j in range(PAIR)]
    lines = [a.T for a in all_gates]
    g = [all_gates[j][:, h : h + 1] for j, h in CHAINS]
    growth = [jnp.exp(g[c]) for c in chains]
    qb = [q_ref[block(j), head_keys(h)] for j, h in CHAINS]
    kb = [k_ref[block(j), head_keys(h)] for j, h in CHAINS]
    dm = [dm_ref[block(j), head_values(h)] for j, h in CHAINS]
    d_p = [
        jnp.where(row >= col, nt(dm[c], d_ref[j, h]), 0.0) for c, (j, h) in enumerate(CHAINS)
    ]
    d_grown = [nt(dm[c], s_ref[j, h]) for c, (j, h) in enumerate(CHAINS)]
    ratio = [decay_ratio(g[c], lines[j][h : h + 1]) for c, (j, h) in enumerate(CHAINS)]
    d_score = [(d_p[c] * ratio[c]).astype(BF16) for c in chains]
    d_q = [mm(d_score[c], kb[c]) + growth[c] * d_grown[c] for c in chains]
    d_cumulative = [jnp.zeros((C, C), F32) for _ in range(PAIR)]
    for c, (j, h) in enumerate(CHAINS):
        dk_ref[j, h] = tn(d_score[c], qb[c])
        flow = d_p[c] * p_ref[j, h].astype(F32)
        d_g = jnp.sum(flow - flow.T, -1, keepdims=True) + jnp.sum(
            d_grown[c] * (qb[c].astype(F32) * growth[c]), -1, keepdims=True
        )
        d_cumulative[j] = jnp.where(col == h, d_g, d_cumulative[j])
    for j in range(PAIR):
        dg_ref[block(j)] = d_cumulative[j]
    window = conv_window(jnp.where(n == 0, edge_ref[...], before_ref[...]), x_ref[...])

    def d_act(act):
        return jnp.concatenate(
            [unit_back(act[:, head_keys(h)], stacked(d_q, h) * DK ** (-0.5)) for h in range(H)],
            1,
        )

    conv_backward(
        n, i, d_act, window, taps_ref[...], carry, dx_ref, tail_ref, front_ref, taps_out_ref
    )


def chunk_backward_kernel(where_ref, *refs):
    along, across, refs = ring_parts(refs[:5]), ring_parts(refs[5:10]), refs[10:]
    y_parts, z_parts, refs = refs[:3], refs[3:6], refs[6:]
    (xk_ref, xv_ref, bk_ref, bv_ref, ek_ref, ev_ref, ab_ref, taps_ref, rates_ref,
     k_ref, v_ref, gates_ref, t_ref, w_ref, u_ref, d_ref, s_ref, pd_ref, qd_ref, dkq_ref,
     dgq_ref,
     dx_ref, tail_ref, front_ref, taps_out_ref, rates_out_ref, state, carry) = refs
    i = pl.program_id(0)
    n = pl.num_programs(0) - 1 - i
    y, z = where_ref[1], where_ref[2]
    row, col = iotas(C, C)
    chains = range(len(CHAINS))

    @pl.when(i == 0)
    def _():
        s = [jnp.zeros((DK, DV), F32) for _ in range(H)]
        for place, maps, parts in ((z, across, z_parts), (y, along, y_parts)):
            for shift in (1, 2, 3):
                for h in range(H):
                    m = maps[shift][h][:, :DK]
                    new = tn_two(m, s[h]) + parts[shift - 1][h].astype(F32)
                    s[h] = jnp.where(place < shift, new, s[h])
        for h in range(H):
            state[h] = s[h]
        carry[...] = jnp.zeros_like(carry)
        taps_out_ref[...] = jnp.zeros_like(taps_out_ref)
        rates_out_ref[...] = jnp.zeros_like(rates_out_ref)

    all_gates = [gates_ref[block(j)] for j in range(PAIR)]
    lines = [a.T for a in all_gates]
    g = [all_gates[j][:, h : h + 1] for j, h in CHAINS]
    beta = [all_gates[j][:, H + h : H + h + 1] for j, h in CHAINS]
    total = [g[c][C - 1 : C] for c in chains]
    growth = [jnp.exp(g[c]) for c in chains]
    fade = [jnp.exp(total[c] - g[c]) for c in chains]
    kb = [k_ref[block(j), head_keys(h)] for j, h in CHAINS]
    k = [a.astype(F32) for a in kb]
    v = [v_ref[block(j), head_values(h)].astype(F32) for j, h in CHAINS]
    held = [s_ref[j, h] for j, h in CHAINS]
    delta = [d_ref[j, h] for j, h in CHAINS]
    w = [w_ref[j, h] for j, h in CHAINS]
    t = [t_ref[j, h] for j, h in CHAINS]
    trail = [k[c] * fade[c] for c in chains]
    old = [None] * len(CHAINS)
    d_delta = [None] * len(CHAINS)
    for c in reversed(chains):
        j, h = CHAINS[c]
        old[c] = state[h]
        d_delta[c] = (pd_ref[j, h] + mm(trail[c], old[c])).astype(BF16)
        state[h] = jnp.exp(total[c]) * old[c] + qd_ref[j, h] - tn(w[c], d_delta[c])
    old_b = [a.astype(BF16) for a in old]
    d_trail = [nt(delta[c], old_b[c]) for c in chains]
    d_w = [nt(d_delta[c], held[c]) for c in chains]
    d_wide_k = [-tn(t[c], d_w[c]) for c in chains]
    d_wide_v = [tn(t[c], d_delta[c]) for c in chains]
    ratio = [decay_ratio(g[c], lines[j][h : h + 1]) for c, (j, h) in enumerate(CHAINS)]
    gram = [nt(kb[c], kb[c]) for c in chains]
    a = [jnp.where(row > col, gram[c] * ratio[c], 0.0) for c in chains]
    d_system = [
        jnp.where(row > col, -(nt(d_wide_k[c], w[c]) + nt(d_wide_v[c], u_ref[j, h])), 0.0)
        for c, (j, h) in enumerate(CHAINS)
    ]
    d_a = [beta[c] * d_system[c] for c in chains]
    d_gram = [d_a[c] * ratio[c] for c in chains]
    both = [(d_gram[c] + d_gram[c].T).astype(BF16) for c in chains]
    d_k = [
        mm(both[c], kb[c])
        + dkq_ref[j, h]
        + (beta[c] * growth[c]) * d_wide_k[c]
        + fade[c] * d_trail[c]
        for c, (j, h) in enumerate(CHAINS)
    ]
    d_v = [beta[c] * d_wide_v[c] for c in chains]
    d_cumulative = [dgq_ref[block(j)] for j in range(PAIR)]
    d_beta = [jnp.zeros((C, C), F32) for _ in range(PAIR)]
    for c, (j, h) in enumerate(CHAINS):
        in_k = jnp.sum(d_wide_k[c] * k[c], -1, keepdims=True) * growth[c]
        in_v = jnp.sum(d_wide_v[c] * v[c], -1, keepdims=True)
        flow = d_a[c] * a[c]
        shed = jnp.sum(d_trail[c] * trail[c], -1, keepdims=True)
        last = jnp.sum(shed, 0, keepdims=True) + jnp.exp(total[c]) * jnp.sum(
            jnp.sum(old[c] * held[c].astype(F32), -1, keepdims=True), 0, keepdims=True
        )
        d_g = (
            jnp.sum(flow - flow.T, -1, keepdims=True)
            + beta[c] * in_k
            - shed
            + jnp.where(row[:, :1] == C - 1, last, 0.0)
        )
        d_b = jnp.sum(d_system[c] * a[c], -1, keepdims=True) + in_v + in_k
        d_cumulative[j] = jnp.where(col == h, d_cumulative[j] + d_g, d_cumulative[j])
        d_beta[j] = jnp.where(col == H + h, d_b, d_beta[j])
    rates = rates_ref[...]
    wide = taps_ref.shape[1]
    for j in range(PAIR):
        d_log = mm_ones((row <= col).astype(F32), d_cumulative[j])
        ab = ab_ref[block(j)]
        slope = rates[0:1] * jax.nn.sigmoid(ab + rates[1:2])
        log_decay = rates[0:1] * softplus(ab + rates[1:2])
        rates_out_ref[0:1] += jnp.sum(d_log * slope, 0, keepdims=True)
        rates_out_ref[1:2] += jnp.sum(d_log * log_decay, 0, keepdims=True)
        d_ab = d_log * slope + d_beta[j] * all_gates[j] * (1.0 - all_gates[j])
        dx_ref[block(j), wide : wide + 128] = d_ab.astype(BF16)
        dx_ref[block(j), wide + 128 :] = jnp.zeros((C, dx_ref.shape[1] - wide - 128), BF16)
    window = conv_window(
        jnp.concatenate(
            [
                jnp.where(n == 0, ek_ref[...], bk_ref[...]),
                jnp.where(n == 0, ev_ref[...], bv_ref[...]),
            ],
            1,
        ),
        jnp.concatenate([xk_ref[...], xv_ref[...]], 1),
    )

    def d_act(act):
        return jnp.concatenate(
            [unit_back(act[:, head_keys(h)], stacked(d_k, h)) for h in range(H)]
            + [stacked(d_v, h) for h in range(H)],
            1,
        )

    conv_backward(
        n, i, d_act, window, taps_ref[...], carry, dx_ref, tail_ref, front_ref, taps_out_ref
    )


def join_columns(x, parts, full_ref):
    own, one, top, bottom, three = parts
    half, width = top.shape

    def at(k):
        return pl.ds(pl.multiple_of(lax.rem(x - k + NX, NX) * width, 128), width)

    full_ref[:, at(0)] = own[...]
    full_ref[:, at(1)] = one[...]
    full_ref[:half, at(2)] = top[...]
    full_ref[half:, at(2)] = bottom[...]
    full_ref[:, at(3)] = three[...]


def gather_norm_kernel(place_ref, after_ref, gain_ref, *refs):
    parts, (full_ref, normed_ref) = refs[:5], refs[5:]
    join_columns(place_ref[0], parts, full_ref)
    for i in range(full_ref.shape[0] // 32):
        u = full_ref[i * 32 : (i + 1) * 32].astype(F32)
        r = lax.rsqrt(jnp.mean(u * u, -1, keepdims=True) + EPSILON)
        normed_ref[i * 32 : (i + 1) * 32] = (u * r * gain_ref[...]).astype(BF16)


def gather_kernel(place_ref, *refs):
    join_columns(place_ref[0], refs[:5], refs[5])


def norm_back_kernel(place_ref, after_ref, gain_ref, u_ref, dy_ref, *refs):
    parts, (d_ref, grad_ref, e_ref) = refs[:5], refs[5:]
    join_columns(place_ref[0], parts, e_ref)
    gain = gain_ref[...]
    total = jnp.zeros((8, u_ref.shape[1]), F32)
    for i in range(u_ref.shape[0] // 32):
        at = slice(i * 32, (i + 1) * 32)
        u = u_ref[at].astype(F32)
        e = e_ref[at].astype(F32)
        r = lax.rsqrt(jnp.mean(u * u, -1, keepdims=True) + EPSILON)
        n = u * r
        en = e * n
        d = r * (gain * e - n * jnp.mean(gain * en, -1, keepdims=True))
        d_ref[at] = (dy_ref[at].astype(F32) + d).astype(BF16)
        for j in range(4):
            total = total + en[j * 8 : (j + 1) * 8]
    grad_ref[...] = jnp.sum(total, 0, keepdims=True)


def pack_kernel(plan, place_ref, *refs):
    parts, (shard_ref, send_ref) = refs[:-2], refs[-2:]
    core = place_ref[0]
    first = core == 0
    height = send_ref.shape[0]
    mine = pl.ds(pl.multiple_of(core * height, height), height)
    at = 0
    for which, start, width, padded in plan:
        part = parts[which]
        half = part.shape[1] // NC
        low, high = part[:, start : start + width], part[:, half + start : half + start + width]
        for out, rows, value in (
            (shard_ref, mine, jnp.where(first, low, high)),
            (send_ref, slice(None), jnp.where(first, high, low)),
        ):
            out[rows, at : at + width] = value
            if padded > width:
                out[rows, at + width : at + padded] = jnp.zeros((height, padded - width), BF16)
        at += padded


def place_kernel(plan, ab_at, place_ref, total_ref, got_ref, *outs):
    core = place_ref[0]
    first = core == 0
    height = got_ref.shape[0]
    mine = pl.ds(pl.multiple_of(core * height, height), height)
    for out, cuts in zip(outs, plan):
        half = out.shape[1] // NC
        for start, to, width in cuts:
            own = total_ref[mine, start : start + width].astype(F32)
            got = got_ref[:, start : start + width].astype(F32)
            out[:, to : to + width] = jnp.where(first, own, got)
            out[:, half + to : half + to + width] = jnp.where(first, got, own)
    if ab_at is not None:
        own = total_ref[mine, ab_at : ab_at + 128].astype(F32)
        got = got_ref[:, ab_at : ab_at + 128].astype(F32)
        turned = jnp.concatenate([own, got], 0).T
        own, got = turned[: 2 * H, :height], turned[: 2 * H, height:]
        low, high = jnp.where(first, own, got), jnp.where(first, got, own)
        for out, start in zip(outs[len(plan) :], (0, H)):
            out[:H] = low[start : start + H]
            out[H:] = high[start : start + H]


def mlp_kernel(own_ref, other_ref, w_ref, d_inner_ref, inner_ref, d_gu_ref):
    x = jnp.concatenate([own_ref[...], other_ref[...]], 0)
    prod = mm(x, w_ref[...])
    width = inner_ref.shape[1]
    gate, up, d_inner = prod[:, :width], prod[:, width:], d_inner_ref[...]
    s = jax.nn.sigmoid(gate)
    act = gate * s
    inner_ref[...] = (act * up).astype(BF16)
    d_gu_ref[:, :width] = (d_inner * up * s * (1.0 + gate * (1.0 - s))).astype(BF16)
    d_gu_ref[:, width:] = (d_inner * act).astype(BF16)


def turn_kernel(*refs):
    at = 0
    for piece in refs[:-1]:
        rows = piece.shape[0]
        refs[-1][:, at : at + rows] = piece[...].T
        at += rows


def outer_kernel(plan, has_weights, *refs):
    refs = list(refs)
    j = pl.program_id(0)
    refs.pop(0)
    weight = refs.pop(0) if has_weights else None
    turned = [refs.pop() for pieces in [p for _, _, p, _, _ in plan][::-1] if pieces][::-1]
    acc = refs.pop() if has_weights else None
    out = refs.pop()
    if has_weights:

        @pl.when(j == 0)
        def _():
            acc[...] = jnp.zeros_like(acc)

    for first, count, pieces, has_front, has_weight in plan:
        if pieces:
            left = turned.pop(0)
            parts, refs = refs[:pieces], refs[pieces:]

            @pl.when(j == first)
            def _(left=left, parts=parts):
                turn_kernel(*parts, left)

        else:
            left = refs.pop(0)
        right = refs.pop(0)
        front = refs.pop(0) if has_front else None

        @pl.when((j >= first) & (j < first + count))
        def _(left=left, right=right, front=front, has_weight=has_weight):
            tokens, width = right.shape
            prod = mm(left[:, :tokens], right[...])
            if front is not None:
                prod = prod + mm(left[:, tokens:], front[...])
            out[...] = prod.astype(BF16)
            if has_weight:
                part = prod * weight[...].astype(F32)
                total = part[:, :128]
                for at in range(128, width, 128):
                    total = total + part[:, at : at + 128]
                acc[...] += total


def params(**more):
    return pltpu.CompilerParams(vmem_limit_bytes=VMEM, **more)


SMEM_SPEC = pl.BlockSpec(memory_space=pltpu.SMEM)
VMEM_SPEC = pl.BlockSpec(memory_space=pltpu.VMEM)
ANY_SPEC = pl.BlockSpec(memory_space=pl.ANY)


def whole_call(kernel, out_shape, place, *operands, scratch=(), after=None, flops=0):
    many = isinstance(out_shape, (tuple, list))
    first = [] if place is None else [place]
    first_specs = [] if place is None else [SMEM_SPEC]
    if after is not None:
        first, first_specs = first + [after], first_specs + [ANY_SPEC]
    outs = out_shape if many else [out_shape]
    moved = sum(v.size * v.dtype.itemsize for v in operands)
    moved += sum(o.size * o.dtype.itemsize for o in outs)
    return pl.pallas_call(
        kernel,
        out_shape=out_shape,
        in_specs=first_specs + [VMEM_SPEC] * len(operands),
        out_specs=[VMEM_SPEC] * len(out_shape) if many else VMEM_SPEC,
        scratch_shapes=list(scratch),
        compiler_params=params(),
        cost_estimate=pl.CostEstimate(
            flops=flops or moved, bytes_accessed=moved, transcendentals=0
        ),
    )(*first, *operands)


def sds(shape, dtype):
    return jax.ShapeDtypeStruct(shape, dtype)


def outer_call(pairs, tile, start, into, after=None, weight=None):
    tokens = pairs[0][1].shape[0]
    scratch = []
    fresh = isinstance(into, int)
    some = pairs[0][0]
    height = some[0].shape[1] if isinstance(some, tuple) else some.shape[0]
    shape = (height, into) if fresh else into.shape
    specs, operands, plan = [ANY_SPEC], [after if fresh else into], []
    counts = [right.shape[1] // tile for _, right, _, _ in pairs]
    firsts = [sum(counts[:i]) for i in range(len(pairs))]
    if weight is not None:

        def weight_index(j):
            column = 0
            for (_, _, _, at), first, count in zip(pairs, firsts, counts):
                if at is not None:
                    inside = jnp.clip(j - first, 0, count - 1)
                    column = jnp.where(j >= first, at + inside * tile, column)
            return 0, pl.multiple_of(column, 128)

        specs.append(pl.BlockSpec((pl.Element(height), pl.Element(tile)), weight_index))
        operands.append(weight)
    for (left, right, front, at), first, count in zip(pairs, firsts, counts):

        def index(j, first=first, count=count):
            return 0, jnp.clip(j - first, 0, count - 1)

        pieces = left if isinstance(left, tuple) else (left,)
        for piece in pieces:
            specs.append(pl.BlockSpec(piece.shape, lambda j: (0, 0)))
        specs.append(pl.BlockSpec((tokens, tile), index))
        operands += [*pieces, right]
        if isinstance(left, tuple):
            scratch.append(pltpu.VMEM((height, tokens), BF16))
        if front is not None:
            specs.append(pl.BlockSpec((front.shape[0], tile), index))
            operands.append(front)
        turning = len(pieces) if isinstance(left, tuple) else 0
        plan.append((first, count, turning, front is not None, at is not None))
    out_shape = [sds(shape, BF16)]
    out_specs = [
        pl.BlockSpec((pl.Element(height), pl.Element(tile)), lambda j: (0, pl.multiple_of(start + j * tile, 128)))
    ]
    if weight is not None:
        out_shape.append(sds((height, 128), F32))
        out_specs.append(pl.BlockSpec((height, 128), lambda j: (0, 0)))
    width = sum(counts) * tile
    out = pl.pallas_call(
        partial(outer_kernel, plan, weight is not None),
        out_shape=out_shape,
        grid=(sum(counts),),
        in_specs=specs,
        out_specs=out_specs,
        scratch_shapes=scratch,
        input_output_aliases={} if fresh else {0: 0},
        compiler_params=params(dimension_semantics=("arbitrary",)),
        cost_estimate=pl.CostEstimate(
            flops=2 * tokens * height * width,
            bytes_accessed=2 * height * width + 4 * tokens * height,
            transcendentals=0,
        ),
    )(*operands)
    return out if weight is not None else out[0]


def on_chips(v, target):
    pairs = []
    for z in range(NZ):
        for y in range(NY):
            for c in range(NC):
                to_z, to_y, to_c = target(z, y, c)
                pairs.append(((z * NY + y) * NC + c, (to_z * NY + to_y) * NC + to_c))
    return lax.ppermute(v, "seq", pairs)


def core_swap(v):
    return on_chips(v, lambda z, y, c: (z, y, 1 - c))


def along_y(v, shift):
    return on_chips(v, lambda z, y, c: (z, (y + shift) % NY, c))


def along_z(v, shift):
    return on_chips(v, lambda z, y, c: ((z + shift) % NZ, y, c))


def along_x(v, shift):
    return lax.ppermute(v, "head", [(i, (i + shift) % NX) for i in range(NX)])


def next_chip(v, step):
    count = NZ * NY * NC
    return lax.ppermute(
        v, "seq", [(i, i + NC * step) for i in range(count) if 0 <= i + NC * step < count]
    )


GROUPS = [[c + NC * j for j in range(NZ * NY)] for c in range(NC)]


def gather_chips(shard):
    return lax.all_gather(shard, "seq", axis=0, tiled=True, axis_index_groups=GROUPS)


def scatter_chips(full):
    return lax.psum_scatter(
        full, "seq", scatter_dimension=0, tiled=True, axis_index_groups=GROUPS
    )


def ring_gather(move, v):
    half = v.shape[0] // 2
    one, three = move(v, 1), move(v, -1)
    return v, one, move(one[:half], 1), move(three[half:], -1), three


def ring_direct(move, v):
    return [v] + [move(v, k) for k in (1, 2, 3)]


def reduce_features(rows_in, dot, x):
    half = rows_in.shape[0] // 2
    arrived = core_swap(dot(rows_in[half:]).astype(BF16))
    own = dot(rows_in[:half]).astype(BF16)
    width = own.shape[1] // NX

    def cut(distance):
        at = (0, lax.rem(x + distance, NX) * width)
        mine = lax.dynamic_slice(own, at, (half, width))
        return mine.astype(F32) + lax.dynamic_slice(arrived, at, (half, width)).astype(F32)

    got = [along_x(cut(k).astype(BF16), k) for k in (2, 1, 3)]
    total = cut(0)
    for part in got:
        total = total + part.astype(F32)
    return total


def plain_dot(left_op, right_op):
    return jnp.dot(left_op, right_op, preferred_element_type=F32)


def dot_last(left_op, right_op):
    return lax.dot_general(
        left_op, right_op, (((1,), (1,)), ((), ())), preferred_element_type=F32
    )


def on_device(
    hidden_in, out_grad, norm_attn, w_query, w_key, w_value, conv_query, conv_key, conv_value,
    w_alpha, w_beta, log_rate, rate_bias, w_gate_out, head_norm, w_out, norm_mlp,
    w_mlp_gate, w_mlp_up, w_mlp_down,
):
    seq = lax.axis_index("seq")
    x = lax.axis_index("head")
    core = seq % NC
    chip = seq // NC
    y, z = chip % NY, chip // NY
    first_core = core == 0
    rows, slice_width = hidden_in.shape
    wide = slice_width * NX
    tokens = rows * NC
    steps = tokens // ROWS
    blocks = tokens // C
    keys = H * DK
    vals = H * DV
    ff = w_mlp_gate.shape[1] // NC
    ff_pad = -(-ff // 128) * 128
    qkv = 2 * keys + vals
    qkv_ab = qkv + 128
    place_x = jnp.stack([x]).astype(jnp.int32)
    place_y = jnp.stack([y]).astype(jnp.int32)
    place = jnp.stack([core, y, z]).astype(jnp.int32)
    place_core = jnp.stack([core]).astype(jnp.int32)

    def gathered(parts, plan):
        height, width = parts[0].shape[0], sum(padded for _, _, _, padded in plan)
        shard, send = whole_call(
            partial(pack_kernel, plan),
            [sds((NC * height, width), BF16), sds((height, width), BF16)], place_core, *parts,
        )
        shard = lax.dynamic_update_slice(shard, core_swap(send), ((1 - core) * height, 0))
        return shard, gather_chips(shard)

    ab = jnp.concatenate(
        [w.T[c * H : (c + 1) * H] for c in range(NC) for w in (w_alpha, w_beta)], 0
    ).T
    shard, full = gathered(
        [w_query, w_key, w_value, ab, w_gate_out, w_out.T],
        [
            (0, 0, keys, keys), (1, 0, keys, keys), (2, 0, vals, vals), (3, 0, 2 * H, 128),
            (4, 0, vals, vals), (5, 0, vals, vals),
        ],
    )
    w_gate, w_attn = full[:, qkv_ab : qkv_ab + vals], full[:, qkv_ab + vals :]
    cuts = [(i * 256, min(256, ff - i * 256)) for i in range(ff_pad // 256)]
    later, _ = lax.optimization_barrier(((w_mlp_gate, w_mlp_up, w_mlp_down.T), shard))
    _, full_mlp = gathered(
        later,
        [(which, start, width, 256) for start, width in cuts for which in (0, 1)]
        + [(2, start, width, 256) for start, width in cuts],
    )
    w_gu, w_dn = full_mlp[:, : 2 * ff_pad], full_mlp[:, 2 * ff_pad :]

    gain_one = norm_attn.reshape(1, wide)
    gain_two = norm_mlp.reshape(1, wide)
    full_in, normed_own = whole_call(
        gather_norm_kernel, [sds((rows, wide), BF16)] * 2, place_x, gain_one,
        *ring_gather(along_x, hidden_in), after=gain_one,
    )
    normed_other = core_swap(normed_own)
    halo = next_chip(
        jnp.where(first_core, normed_other[rows - 16 :], normed_own[rows - 16 :]), 1
    )
    normed = jnp.concatenate([normed_own, normed_other, halo], 0)
    dy_own = whole_call(
        gather_kernel, sds((rows, wide), BF16), place_x,
        *ring_gather(along_x, out_grad),
    )
    dy_other = core_swap(dy_own)
    full_dy = jnp.concatenate([dy_own, dy_other], 0)
    normed_t = whole_call(
        turn_kernel, sds((wide, tokens + 16), BF16), None, normed_own, normed_other, halo
    )
    dy_t = whole_call(turn_kernel, sds((wide, tokens), BF16), None, dy_own, dy_other)
    normed, full_dy, normed_t, dy_t = lax.optimization_barrier((normed, full_dy, normed_t, dy_t))

    proj = plain_dot(normed, full[:, :qkv_ab])
    gate_in = plain_dot(normed, w_gate)

    def conv_half(w):
        width = w.shape[1] // NC
        return lax.dynamic_slice_in_dim(w, core * width, width, 1)

    taps_all = jnp.pad(
        jnp.concatenate(
            [conv_half(conv_query), conv_half(conv_key), conv_half(conv_value)], 1
        ).astype(F32),
        ((0, 8 - TAPS), (0, 0)),
    )
    rate_rows = jnp.stack([-jnp.exp(log_rate), rate_bias])
    rates = jnp.pad(
        lax.dynamic_slice_in_dim(rate_rows, core * H, H, 1), ((0, 6), (0, 128 - H))
    )
    head_gain = head_norm.reshape(1, DV)

    def at(n, where):
        return lax.rem(n + steps // NC * where[0], steps)

    def rows_spec(width, backward=False, col=0):
        if backward:
            return pl.BlockSpec((ROWS, width), lambda i, s: (at(steps - 1 - i, s), col))
        return pl.BlockSpec((ROWS, width), lambda i, s: (at(i, s), col))

    def before_spec(width, backward=False, col=0):
        def index(i, s):
            n = steps - 1 - i if backward else i
            return (at(jnp.maximum(n - 1, 0), s) * (ROWS // 16) + ROWS // 16 - 1, col)

        return pl.BlockSpec((16, width), index)

    def chain_spec(cols, backward=False):
        if backward:
            return pl.BlockSpec((PAIR, H, C, cols), lambda i, s: (steps - 1 - i, 0, 0, 0))
        return pl.BlockSpec((PAIR, H, C, cols), lambda i, s: (i, 0, 0, 0))

    def full_spec(*shape):
        zeros = (0,) * len(shape)
        return pl.BlockSpec(shape, lambda i, s: zeros)

    edge_spec = pl.BlockSpec((16, qkv), lambda i, s: (tokens // 16, 0))

    def chunk_call(kernel, in_specs, outs, scratch, *operands):
        return pl.pallas_call(
            kernel,
            out_shape=[o for o, _ in outs],
            grid_spec=pltpu.PrefetchScalarGridSpec(
                num_scalar_prefetch=1,
                grid=(steps,),
                in_specs=in_specs,
                out_specs=[spec for _, spec in outs],
                scratch_shapes=scratch,
            ),
            compiler_params=params(dimension_semantics=("arbitrary",)),
        )(place, *operands)

    map_shape, part_shape = (DK, DK + DV), (DK, DV)
    q_n, k_n, v_n, gates, p_c, t_c, w_c, u_c, own_map = chunk_call(
        chunk_forward_kernel,
        [
            rows_spec(qkv), before_spec(qkv), edge_spec, rows_spec(128, col=qkv // 128),
            full_spec(8, qkv), full_spec(8, 128),
        ],
        [
            (sds((tokens, keys), BF16), rows_spec(keys)),
            (sds((tokens, keys), BF16), rows_spec(keys)),
            (sds((tokens, vals), BF16), rows_spec(vals)),
            (sds((tokens, 128), F32), rows_spec(128)),
            (sds((blocks, H, C, C), BF16), chain_spec(C)),
            (sds((blocks, H, C, C), BF16), chain_spec(C)),
            (sds((blocks, H, C, DK), BF16), chain_spec(DK)),
            (sds((blocks, H, C, DV), F32), chain_spec(DV)),
            (sds((H,) + map_shape, BF16), full_spec(H, *map_shape)),
        ],
        [pltpu.VMEM((H,) + map_shape, F32)],
        proj, proj, proj, proj, taps_all, rates,
    )
    y_maps = ring_gather(along_y, own_map)
    line_map = whole_call(
        line_map_kernel, sds((H,) + map_shape, BF16), place_y, *y_maps,
        scratch=[pltpu.VMEM((NY, H) + map_shape, BF16)],
    )
    z_maps = ring_gather(along_z, line_map)
    map_specs = [full_spec(h, *map_shape) for h in (H, H, 1, 1, H)] * 2
    mixed, attn, d_c, s_c = chunk_call(
        chunk_output_kernel,
        map_specs
        + [
            rows_spec(keys), rows_spec(keys), rows_spec(128), chain_spec(C), chain_spec(DK),
            chain_spec(DV), rows_spec(vals), full_spec(1, DV),
        ],
        [
            (sds((tokens, vals), F32), rows_spec(vals)),
            (sds((tokens, vals), BF16), rows_spec(vals)),
            (sds((blocks, H, C, DV), BF16), chain_spec(DV)),
            (sds((blocks, H, DK, DV), BF16), chain_spec(DV)),
        ],
        [pltpu.VMEM((H,) + part_shape, F32)],
        *y_maps, *z_maps, q_n, k_n, gates, p_c, w_c, u_c, gate_in, head_gain,
    )
    attn_part = reduce_features(attn, lambda v: dot_last(v, w_attn), x)
    middle = (hidden_in.astype(F32) + attn_part).astype(BF16)

    d_inner = plain_dot(full_dy, w_dn)
    full_middle, normed_two_own = whole_call(
        gather_norm_kernel, [sds((rows, wide), BF16)] * 2, place_x, gain_two,
        *ring_gather(along_x, middle), after=d_inner,
    )
    normed_two_other = core_swap(normed_two_own)
    inner, d_gu = pl.pallas_call(
        mlp_kernel,
        out_shape=[sds((tokens, ff_pad), BF16), sds((tokens, 2 * ff_pad), BF16)],
        grid=(ff_pad // 256,),
        in_specs=[
            pl.BlockSpec((rows, wide), lambda j: (0, 0)),
            pl.BlockSpec((rows, wide), lambda j: (0, 0)),
            pl.BlockSpec((wide, 512), lambda j: (0, j)),
            pl.BlockSpec((tokens, 256), lambda j: (0, j)),
        ],
        out_specs=[
            pl.BlockSpec((tokens, 256), lambda j: (0, j)),
            pl.BlockSpec((tokens, 512), lambda j: (0, j)),
        ],
        compiler_params=params(dimension_semantics=("arbitrary",)),
    )(normed_two_own, normed_two_other, full_mlp, d_inner)
    d_two = reduce_features(d_gu, lambda v: dot_last(v, w_gu), x)
    mlp_grads = outer_call(
        [((normed_two_own, normed_two_other), d_gu, None, None), (dy_t, inner, None, None)],
        256, 0, 3 * ff_pad,
        after=d_gu,
    )
    mlp_grads, d_two = lax.optimization_barrier((mlp_grads, d_two))
    mlp_summed = scatter_chips(mlp_grads)
    d_middle_own, grad_norm_mlp = whole_call(
        norm_back_kernel, [sds((rows, wide), BF16), sds((1, wide), F32)], place_x,
        gain_two, full_middle, dy_own, *ring_gather(along_x, d_two.astype(BF16)),
        scratch=[pltpu.VMEM((rows, wide), BF16)], after=mlp_grads,
    )
    d_middle_other = core_swap(d_middle_own)

    wa_spec = pl.BlockSpec(
        (pl.Element(wide), pl.Element(vals)), lambda i, s: (0, qkv_ab + vals)
    )
    dm, d_gate_in, grad_head_norm, p_dm, q_dm, own_part = chunk_call(
        chunk_adjoint_kernel,
        [
            full_spec(rows, wide), full_spec(rows, wide), wa_spec,
            rows_spec(vals, True), rows_spec(vals, True), full_spec(1, DV),
            rows_spec(keys, True), rows_spec(keys, True), rows_spec(128, True),
            chain_spec(C, True), chain_spec(DK, True),
        ],
        [
            (sds((tokens, vals), BF16), rows_spec(vals, True)),
            (sds((tokens, vals), BF16), rows_spec(vals, True)),
            (sds((8, DV), F32), full_spec(8, DV)),
            (sds((blocks, H, C, DV), F32), chain_spec(DV, True)),
            (sds((blocks, H, DK, DV), F32), chain_spec(DV, True)),
            (sds((H,) + part_shape, BF16), full_spec(H, *part_shape)),
        ],
        [pltpu.VMEM((H,) + part_shape, F32)],
        d_middle_own, d_middle_other, full, mixed, gate_in, head_gain, q_n, k_n, gates, p_c, w_c,
    )
    y_parts = ring_direct(along_y, own_part)
    taps_q, taps_kv = taps_all[:, :keys], taps_all[:, keys:]
    kv = keys + vals

    def window_specs(width, col):
        return [
            rows_spec(width, True, col), before_spec(width, True, col),
            pl.BlockSpec((16, width), lambda i, s: (tokens // 16, col)),
        ]

    d_xq, tail_q, front_q, grad_taps_q, d_kq, d_gq = chunk_call(
        chunk_query_kernel,
        window_specs(keys, 0)
        + [
            full_spec(8, keys), rows_spec(keys, True), rows_spec(keys, True),
            rows_spec(128, True), chain_spec(C, True), chain_spec(DV, True),
            chain_spec(DV, True), rows_spec(vals, True),
        ],
        [
            (sds((tokens, keys), BF16), rows_spec(keys, True)),
            (sds((16, keys), F32), full_spec(16, keys)),
            (sds((16, keys), F32), full_spec(16, keys)),
            (sds((8, keys), F32), full_spec(8, keys)),
            (sds((blocks, H, C, DK), F32), chain_spec(DK, True)),
            (sds((tokens, 128), F32), rows_spec(128, True)),
        ],
        [pltpu.VMEM((8, keys), F32)],
        proj, proj, proj, taps_q, q_n, k_n, gates, p_c, d_c, s_c, dm,
    )
    line_part = whole_call(
        line_adjoint_kernel, sds((H,) + part_shape, BF16), place_y, *y_maps, *y_parts,
        scratch=[
            pltpu.VMEM((NY, H, DK, DK), BF16), pltpu.VMEM((NY, H) + part_shape, BF16),
        ],
    )
    z_parts = ring_direct(along_z, line_part)
    rest = kv + 256
    some_grads, gain_a = outer_call(
        [
            (normed_t, d_xq, front_q, 0), (normed_t, d_gate_in, None, qkv_ab),
            ((d_middle_own, d_middle_other), attn, None, None),
        ],
        256, rest, rest + keys + 2 * vals, after=own_part, weight=full,
    )
    part_specs = [full_spec(H, *part_shape)] * 6
    x_specs = [spec for pair in zip(window_specs(keys, 1), window_specs(vals, 1)) for spec in pair]
    d_xkv, tail, front, grad_taps_kv, grad_rates = chunk_call(
        chunk_backward_kernel,
        map_specs
        + part_specs
        + x_specs
        + [
            rows_spec(128, True, qkv // 128), full_spec(8, kv), full_spec(8, 128),
            rows_spec(keys, True), rows_spec(vals, True), rows_spec(128, True),
            chain_spec(C, True), chain_spec(DK, True), chain_spec(DV, True),
            chain_spec(DV, True), chain_spec(DV, True), chain_spec(DV, True),
            chain_spec(DV, True), chain_spec(DK, True), rows_spec(128, True),
        ],
        [
            (sds((tokens, rest), BF16), rows_spec(rest, True)),
            (sds((16, kv), F32), full_spec(16, kv)),
            (sds((16, kv), F32), full_spec(16, kv)),
            (sds((8, kv), F32), full_spec(8, kv)),
            (sds((8, 128), F32), full_spec(8, 128)),
        ],
        [pltpu.VMEM((H,) + part_shape, F32), pltpu.VMEM((8, kv), F32)],
        *y_maps, *z_maps, *y_parts[1:], *z_parts[1:],
        proj, proj, proj, proj, proj, proj, proj, taps_kv, rates, k_n, v_n, gates, t_c, w_c, u_c,
        d_c, s_c, p_dm, q_dm, d_kq, d_gq,
    )

    last_grads, gain_b = outer_call(
        [(normed_t, d_xkv, jnp.pad(front, ((0, 0), (0, rest - kv))), keys)], 256, 0, some_grads,
        weight=full,
    )
    summed = scatter_chips(last_grads)
    norm_attn_part = jnp.sum(gain_a + gain_b, 1) / norm_attn

    fixed = jnp.concatenate([tail_q, tail], 1) + next_chip(
        jnp.concatenate([front_q, front], 1), -1
    )
    last_at = jnp.where(first_core, tokens - 16, rows - 16)
    d_all = lax.dynamic_update_slice(
        jnp.concatenate([d_xq, d_xkv[:, : kv + 128], d_gate_in], 1), fixed.astype(BF16), (last_at, 0)
    )
    d_one = reduce_features(
        d_all, lambda v: dot_last(v, full[:, : qkv_ab + vals]), x
    )
    u = full_in.astype(F32)
    factor = lax.rsqrt(jnp.mean(u * u, -1, keepdims=True) + EPSILON)
    own_gain = lax.dynamic_slice_in_dim(gain_one, x * slice_width, slice_width, 1)
    n_own = hidden_in.astype(F32) * factor
    row_sum = jnp.sum(d_one * n_own * own_gain, -1).reshape(2, rows // 2)
    row_sum = row_sum + (along_x(row_sum, 1) + along_x(row_sum, 2) + along_x(row_sum, 3))
    row_mean = row_sum.reshape(rows, 1) / wide
    d_middle_cols = lax.dynamic_slice_in_dim(d_middle_own, x * slice_width, slice_width, 1)
    grad_input = (
        d_middle_cols.astype(F32) + factor * (d_one * own_gain - n_own * row_mean)
    ).astype(BF16)
    inner_late, _ = lax.optimization_barrier((inner, d_one))
    mlp_part = reduce_features(inner_late, lambda v: dot_last(v, w_dn), x)
    output = (middle.astype(F32) + mlp_part).astype(BF16)

    def placed(v, index, count):
        return jnp.where(jnp.arange(count).reshape((count,) + (1,) * v.ndim) == index, v[None], 0.0)

    shared = jnp.concatenate([norm_attn_part, grad_head_norm[0]]).reshape(-1, 128)
    shared = shared + (along_x(shared, 1) + along_x(shared, 2) + along_x(shared, 3))
    per_core = placed(
        jnp.concatenate(
            [
                jnp.concatenate([grad_taps_q, grad_taps_kv], 1)[:TAPS].reshape(-1),
                grad_rates[:2].reshape(-1),
            ]
        ),
        core, NC,
    ).reshape(-1, 128)
    split_a = shared.shape[0]
    split_b = split_a + per_core.shape[0]
    small = jnp.concatenate([shared, per_core, grad_norm_mlp.reshape(-1, 128)], 0)
    small = small + core_swap(small)
    small = small + (along_y(small, 1) + along_y(small, 2) + along_y(small, 3))
    small = small + (along_z(small, 1) + along_z(small, 2) + along_z(small, 3))
    grad_norm_attn = small[:split_a].reshape(-1)[:wide]
    grad_head_norm = small[:split_a].reshape(-1)[wide : wide + DV]
    cores = small[split_a:split_b].reshape(NC, -1)
    conv = cores[:, : TAPS * qkv].reshape(NC, TAPS, qkv)
    rate_sums = cores[:, TAPS * qkv :].reshape(NC, 2, 128)[:, :, :H]

    def joined(part):
        return jnp.swapaxes(part, 0, 1).reshape(TAPS, -1)

    grad_conv_query = joined(conv[:, :, :keys])
    grad_conv_key = joined(conv[:, :, keys : 2 * keys])
    grad_conv_value = joined(conv[:, :, 2 * keys :])
    grad_rate_bias = rate_sums[:, 0].reshape(-1)
    grad_log_rate = rate_sums[:, 1].reshape(-1)
    grad_norm_mlp = small[split_b:].reshape(-1)

    def placed_rows(total, plan, ab_at=None):
        height = total.shape[0] // NC
        got = core_swap(lax.dynamic_slice_in_dim(total, (1 - core) * height, height, 0))
        shapes = [sds((height, NC * width), F32) for width, _ in plan]
        if ab_at is not None:
            shapes += [sds((NC * H, height), F32)] * 2
        return whole_call(
            partial(place_kernel, [cuts for _, cuts in plan], ab_at), shapes, place_core, total,
            got,
        )

    grad_mlp_gate, grad_mlp_up, grad_down_t = placed_rows(
        mlp_summed,
        [
            (ff, [(2 * start, start, width) for start, width in cuts]),
            (ff, [(2 * start + 256, start, width) for start, width in cuts]),
            (ff, [(2 * ff_pad, 0, ff)]),
        ],
    )
    done = (
        output, grad_input, grad_norm_attn, grad_conv_query, grad_conv_key, grad_conv_value,
        grad_log_rate, grad_rate_bias, grad_head_norm, grad_norm_mlp, grad_mlp_gate, grad_mlp_up,
        grad_down_t,
    )
    summed, done = lax.optimization_barrier((summed, done))
    (
        output, grad_input, grad_norm_attn, grad_conv_query, grad_conv_key, grad_conv_value,
        grad_log_rate, grad_rate_bias, grad_head_norm, grad_norm_mlp, grad_mlp_gate, grad_mlp_up,
        grad_down_t,
    ) = done
    grad_key, grad_value, grad_query, grad_gate_out, grad_out_t, grad_alpha_t, grad_beta_t = (
        placed_rows(
            summed,
            [
                (keys, [(0, 0, keys)]), (vals, [(keys, 0, vals)]), (keys, [(rest, 0, keys)]),
                (vals, [(rest + keys, 0, vals)]), (vals, [(rest + keys + vals, 0, vals)]),
            ],
            kv,
        )
    )
    grad_alpha, grad_beta = grad_alpha_t.T, grad_beta_t.T
    grad_mlp_down, grad_out = grad_down_t.T, grad_out_t.T
    return (
        output, grad_input, grad_norm_attn, grad_query, grad_key, grad_value,
        grad_conv_query, grad_conv_key, grad_conv_value, grad_alpha, grad_beta,
        grad_log_rate, grad_rate_bias, grad_gate_out, grad_head_norm, grad_out,
        grad_norm_mlp, grad_mlp_gate, grad_mlp_up, grad_mlp_down,
    )


def solution(mesh):
    rows, columns = P("seq", "head"), P("head", "seq")
    taps, heads, whole = P(None, "head"), P("head"), P()
    return jax.shard_map(
        on_device,
        mesh=mesh,
        in_specs=(
            rows, rows, whole, rows, rows, rows, taps, taps, taps, rows, rows, heads, heads,
            rows, whole, columns, whole, rows, rows, columns,
        ),
        out_specs=(
            rows, rows, whole, rows, rows, rows, taps, taps, taps, rows, rows, heads, heads,
            rows, whole, columns, whole, rows, rows, columns,
        ),
        check_vma=False,
    )
```

time: 2020 us -> 451 us (0.22)
  waiting for transfers between devices: 884 us -> 132 us
  matrix products: 426 us -> 43.1 us
  other arithmetic: 280 us -> 21.5 us
  blocking collectives: 187 us -> 0 us
  local copies, waits for them, and re-layouts: 197 us -> 24.8 us
  Pallas kernels: 0 us -> 124 us
  starting transfers between devices: 18.4 us -> 83.1 us
    all_gather x16 -> x2, waiting for transfers between devices: 448 us -> 17.9 us  [gather_chips(): lax.all_gather(shard, 'seq', axis=0, tiled=True, axis_index_groups=GROUPS)]
    dot_general x200 -> x3, matrix products: 373 us -> 16.1 us  [plain_dot(): return jnp.dot(left_op, right_op, preferred_element_type=F32)]
    another operation x74 -> x3, other arithmetic: 185 us -> 0.6 us  [the longest x1 0.59 us: on_device(): place = jnp.stack([core, y, z]).astype(jnp.int32)]
    reduce_scatter x10 -> x2, waiting for transfers between devices: 186 us -> 0.85 us  [scatter_chips(): lax.psum_scatter(full, 'seq', scatter_dimension=0, tiled=True, axis_index...]
    unnamed x32 -> x4, waiting for transfers between devices: 163 us -> 0.07 us
    psum x2 -> x0, blocking collectives: 138 us -> none  [the longest x1 127 us: on_device(): lax.psum(grad_norm_attn.astype(jnp.bfloat16), 'seq').astype(jnp.float32)]
    pallas_call x0 -> x21, Pallas kernels: none -> 124 us  [the longest x5 49.3 us: chunk_call(): pl.pallas_call(kernel, out_shape=[o for o, _ in outs], grid_spec=pltpu.Pr...]
    ppermute x2 -> x69, waiting for transfers between devices: 0.01 us -> 113 us  [the longest x34 63.8 us: along_x(): return lax.ppermute(v, 'head', [(i, (i + shift) % NX) for i in range(NX)])]
  transfers between devices with their start and end apart: 32 -> 73, of which waited for: 20 -> 43; matrix products, arithmetic and copies ran while one was open for 32% -> 16% of each run, Pallas kernels for 0% -> 25%
where the time goes in v1:
time: 451 us; the launch traced here: 444 us
  waiting for transfers between devices  132 us (29%)
  Pallas kernels  124 us (27%)
  starting transfers between devices  83.1 us (18%)
  matrix products  43.1 us (10%)
  local copies, waits for them, and re-layouts  24.8 us (5%)
  other arithmetic  21.5 us (5%)
  between operations  15 us (3%)
    ppermute x34, waiting for transfers between devices, along_x(): return lax.ppermute(v, 'head', [(i, (i + shift) % NX) for i in range(NX)])  63.8 us
    ppermute x34, starting transfers between devices, along_x(): return lax.ppermute(v, 'head', [(i, (i + shift) % NX) for i in range(NX)])  50.5 us
    pallas_call x5, Pallas kernels, chunk_call(): pl.pallas_call(kernel, out_shape=[o for o, _ in outs], grid_spec=pltpu.Pr...  49.3 us
    ppermute x33, waiting for transfers between devices, on_chips(): return lax.ppermute(v, 'seq', pairs)  48.9 us
    pallas_call x12, Pallas kernels, whole_call(): pl.pallas_call(kernel, out_shape=out_shape, in_specs=first_specs + [VMEM_...  35.1 us
    pallas_call x3, Pallas kernels, outer_call(): pl.pallas_call(partial(outer_kernel, plan, weight is not None), out_shape...  32 us
    ppermute x33, starting transfers between devices, on_chips(): return lax.ppermute(v, 'seq', pairs)  27.4 us
    dot_general x8, matrix products, dot_last(): lax.dot_general(left_op, right_op, (((1,), (1,)), ((), ())), preferred_el...  27.1 us
  transfers between devices with their start and end apart: 73, of which 43 were waited for; matrix products, arithmetic and copies ran while one was open for 16% of the time, Pallas kernels for 25%

profile of v1, /device:TPU:0, one launch (start us, length us, event | category | flops | bytes accessed | tf_op | source)
XLA Modules:
  0.0 443.5 jit_solution(16066759364363725972)
XLA Ops:
  21.7 5.9 %collective-permute-done.2.refs_4_ = bf16[256,512]{1,0:T(8,128)(2,1)S(1)} collective-permute-done((bf16[256,512]{1,0:T(8,128)(2,1)S(1)}, bf16[256,512]{1,0:T(8,128)(2,1)S(1)}, u32[]{:S(2)}, u32[]{:S(2)}) %collective-permute-start.2) | collective-permute-done | bytes 262176 | tf_op jit(solution)/shard_map/ppermute | solution.py:829
  27.7 3.8 collective-permute-start.3
  34.8 4.3 collective-permute-done.1.refs_2_
  67.7 3.9 shard_map.349.refs_2_.refs_5_
  72.6 17.9 %all-gather.5.cloned.1.call-done.wa_ref.refs_1_ = bf16[2048,2176]{1,0:T(8,128)(2,1)} async-done(((bf16[128,2176]{1,0:T(8,128)(2,1)}), bf16[2048,2176]{1,0:T(8,128)(2,1)}) %all-gather.5.cloned.1.call-update) | async-done | bytes 8912912 | tf_op jit(solution)/shard_map/all_gather | solution.py:843
  90.5 6.7 %fusion.8.x_ref.before_ref.edge_ref.ab_ref.refs_16_.refs_17_.refs_18_.refs_19_.refs_20_.refs_21_.refs_22_ = f32[528,1152]{1,0:T(8,128)} fusion(bf16[528,2048]{1,0:T(8,128)(2,1)S(1)} %pad_maximum_fusion, bf16[2048,2176]{1,0:T(8,128)(2,1)} %all-gather.5.cloned.1.call-done.wa_ref.refs_1_), kind=kOutput, calls=%fused_computation.8 | convolution fusion | flops 2491416576 | bytes 9314304 | tf_op jit(solution)/shard_map/dot_general | solution.py:881
  97.3 12.4 %shard_map.353 = (bf16[512,256]{1,0:T(8,128)(2,1)}, bf16[512,256]{1,0:T(8,128)(2,1)}, bf16[512,512]{1,0:T(8,128)(2,1)}, f32[512,128]{1,0:T(8,128)}, bf16[4,2,128...) custom-call(s32[3]{0:T(128)} %pad_add_fusion.where_ref, ...), custom_call_target="tpu_custom_call" | custom-call | tf_op jit(solution)/shard_map/pallas_call | solution.py:1015
  111.8 8.1 %collective-permute-done.15.refs_4_ = bf16[2,128,384]{2,1,0:T(8,128)(2,1)S(1)} collective-permute-done((bf16[2,128,384]{2,1,0:T(8,128)(2,1)}, bf16[2,128,384]{2,1,0:T(8,128)(2,1)S(1)}, u32[]{:S(2)}, u32[]{:S(2)}) %collective-permute-start.15) | collective-permute-done | bytes 196640 | tf_op jit(solution)/shard_map/ppermute | solution.py:813
  134.5 8.8 %collective-permute-done.19.refs_9_ = bf16[2,128,384]{2,1,0:T(8,128)(2,1)S(1)} collective-permute-done((bf16[2,128,384]{2,1,0:T(8,128)(2,1)}, bf16[2,128,384]{2,1,0:T(8,128)(2,1)S(1)}, u32[]{:S(2)}, u32[]{:S(2)}) %collective-permute-start.19) | collective-permute-done | bytes 196640 | tf_op jit(solution)/shard_map/ppermute | solution.py:813
  147.4 3.9 fusion.26.refs_16_.gate_ref
  151.3 4.0 collective-permute-done.18.refs_7_
  155.9 7.3 %shard_map.355 = (f32[512,512]{1,0:T(8,128)}, bf16[512,512]{1,0:T(8,128)(2,1)}, bf16[4,2,128,256]{3,2,1,0:T(8,128)(2,1)}, bf16[4,2,128,256]{3,2,1,0:T(8,128)(2,1)}) custom-call(s32[3]{0:T(128)} %pad_add_fusion.where_ref, bf16[2,128,384]{2,1,0:T(8,128)(2,1)} %get-tuple-element.110.refs_0_, bf16[2,128,384]{2,1,0:T(8,128)(2,1)} %copy-done.10, ...), custom_call_target="tpu_custom_call" | custom-call | tf_op jit(solution)/shard_map/pallas_call | solution.py:1015
  174.6 5.7 %collective-permute-done.22 = bf16[256,512]{1,0:T(8,128)(2,1)S(1)} collective-permute-done((bf16[256,512]{1,0:T(8,128)(2,1)S(1)}, bf16[256,512]{1,0:T(8,128)(2,1)S(1)}, u32[]{:S(2)}, u32[]{:S(2)}) %collective-permute-start.22) | collective-permute-done | bytes 262176 | tf_op jit(solution)/shard_map/ppermute | solution.py:829
  180.3 5.2 %collective-permute-done.24 = bf16[256,512]{1,0:T(8,128)(2,1)S(1)} collective-permute-done((bf16[256,512]{1,0:T(8,128)(2,1)S(1)}, bf16[256,512]{1,0:T(8,128)(2,1)S(1)}, u32[]{:S(2)}, u32[]{:S(2)}) %collective-permute-start.24) | collective-permute-done | bytes 262176 | tf_op jit(solution)/shard_map/ppermute | solution.py:829
  189.4 5.8 %collective-permute-done.27.refs_4_ = bf16[256,512]{1,0:T(8,128)(2,1)S(1)} collective-permute-done((bf16[256,512]{1,0:T(8,128)(2,1)S(1)}, bf16[256,512]{1,0:T(8,128)(2,1)S(1)}, u32[]{:S(2)}, u32[]{:S(2)}) %collective-permute-start.27) | collective-permute-done | bytes 262176 | tf_op jit(solution)/shard_map/ppermute | solution.py:829
  199.0 5.5 %fusion.24.after_ref.d_inner_ref = f32[512,768]{1,0:T(8,128)} fusion(bf16[512,2048]{1,0:T(8,128)(2,1)} %pad_maximum_fusion.1, bf16[2048,2304]{1,0:T(8,128)(2,1)} %all-gather.3.cloned.1.call-done.w_ref), kind=kOutput, calls=%fused_computation.20 | convolution fusion | flops 1610612736 | bytes 6815744 | tf_op jit(solution)/shard_map/dot_general | solution.py:881
  212.5 8.1 %shard_map.357 = (bf16[512,768]{1,0:T(8,128)(2,1)}, bf16[512,1536]{1,0:T(8,128)(2,1)}) custom-call(bf16[256,2048]{1,0:T(8,128)(2,1)} %get-tuple-element.118.own_ref.refs_1_, bf16[256,2048]{1,0:T(8,128)(2,1)} %copy-done.20, bf16[2048,2304]{1,0:T(8,128)(2,1)} %all-gather.3.cloned.1.call-done.w_ref, f32[512,768]{1,0:T(8,128)} %fusion.24.after_ref.d_inner_ref), custom_call_target="tpu_custom_call" | custom-call | tf_op jit(solution)/shard_map/pallas_call | solution.py:1081
  220.7 5.0 %fusion.19 = bf16[256,2048]{1,0:T(8,128)(2,1)S(1)} fusion(bf16[2048,2304]{1,0:T(8,128)(2,1)} %all-gather.3.cloned.1.call-done.w_ref, bf16[512,1536]{1,0:T(8,128)(2,1)} %get-tuple-element.119.refs_0_.refs_3_), kind=kOutput, calls=%fused_computation.15 | convolution fusion | flops 1611137024 | bytes 8126464 | tf_op jit(solution)/shard_map/dot_general | solution.py:885
  232.5 12.4 %shard_map.358.after_ref = bf16[2048,2304]{1,0:T(8,128)(2,1)} custom-call(bf16[512,1536]{1,0:T(8,128)(2,1)} %get-tuple-element.119.refs_0_.refs_3_, bf16[256,2048]{1,0:T(8,128)(2,1)} %get-tuple-element.118.own_ref.refs_1_, bf16[256,2048]{1,0:T(8,128)(2,1)} %copy-done.20, bf16[512,1536]{1,0:T(8,128)(2,1)} %get-tuple-element.119.refs_0_.refs_3_, ...), custom_call_target="tpu_custom_call" | custom-call | flops 4831838208 | bytes 13631488 | tf_op jit(solution)/shard_map/pallas_call | solution.py:788
  248.9 5.3 %collective-permute-done.36.refs_4_ = bf16[256,512]{1,0:T(8,128)(2,1)S(1)} collective-permute-done((bf16[256,512]{1,0:T(8,128)(2,1)S(1)}, bf16[256,512]{1,0:T(8,128)(2,1)S(1)}, u32[]{:S(2)}, u32[]{:S(2)}) %collective-permute-start.36) | collective-permute-done | bytes 262176 | tf_op jit(solution)/shard_map/ppermute | solution.py:829
  264.8 4.5 %shard_map.359 = (bf16[256,2048]{1,0:T(8,128)(2,1)}, f32[1,2048]{1,0:T(1,128)}) custom-call(s32[1]{0:T(128)} %bitcast.3.place_ref, bf16[2048,2304]{1,0:T(8,128)(2,1)} %shard_map.358.after_ref, f32[1,2048]{1,0:T(1,128)} %bitcast.83, bf16[256,2048]{1,0:T(8,128)(2,1)} %get-tuple-element.123.u_ref, bf16[256,2048]{1,0:T(8,128)(2,1)} %shard_map.348.refs_0_.dy_ref, ...), custom_call_target="tpu_custom_call" | custom-call | flops 4210688 | bytes 4210688 | tf_op jit(solution)/shard_map/pallas_call | solution.py:724
  273.2 9.0 %shard_map.360 = (bf16[512,512]{1,0:T(8,128)(2,1)}, bf16[512,512]{1,0:T(8,128)(2,1)}, f32[8,256]{1,0:T(8,128)}, f32[4,2,128,256]{3,2,1,0:T(8,128)}, f32[4,2,128,...) custom-call(s32[3]{0:T(128)} %pad_add_fusion.where_ref, bf16[256,2048]{1,0:T(8,128)(2,1)} %get-tuple-element.125.own_ref.refs_7_, ...), custom_call_target="tpu_custom_call" | custom-call | tf_op jit(solution)/shard_map/pallas_call | solution.py:1015
  285.5 5.5 %shard_map.361 = (bf16[512,256]{1,0:T(8,128)(2,1)}, f32[16,256]{1,0:T(8,128)}, f32[16,256]{1,0:T(8,128)}, f32[8,256]{1,0:T(8,128)}, f32[4,2,128,128]{3,2,1,0:T(8,128)}, /*index=5*/f32[512,128]{1,0:T(8,128)}) custom-call(s32[3]{0:T(128)} %pad_add_fusion.where_ref, ...), custom_call_target="tpu_custom_call" | custom-call | tf_op jit(solution)/shard_map/pallas_call | solution.py:1015
  302.1 11.0 %shard_map.362 = (bf16[2048,2304]{1,0:T(8,128)(2,1)}, f32[2048,128]{1,0:T(8,128)}) custom-call(bf16[2,128,256]{2,1,0:T(8,128)(2,1)} %get-tuple-element.127.refs_0_.refs_5_, bf16[2048,2176]{1,0:T(8,128)(2,1)} %all-gather.5.cloned.1.call-done.wa_ref.refs_1_, bf16[2048,528]{1,0:T(8,128)(2,1)} %shard_map.349.refs_2_.refs_5_, ...), custom_call_target="tpu_custom_call" | custom-call | flops 2684354560 | bytes 9437184 | tf_op jit(solution)/shard_map/pallas_call | solution.py:788
  313.9 15.1 %shard_map.364 = (bf16[512,1024]{1,0:T(8,128)(2,1)}, f32[16,768]{1,0:T(8,128)}, f32[16,768]{1,0:T(8,128)}, f32[8,768]{1,0:T(8,128)}, f32[8,128]{1,0:T(8,128)}) custom-call(s32[3]{0:T(128)} %pad_add_fusion.where_ref, bf16[2,128,384]{2,1,0:T(8,128)(2,1)} %get-tuple-element.110.refs_0_, bf16[2,128,384]{2,1,0:T(8,128)(2,1)} %copy-done.10, ...), custom_call_target="tpu_custom_call" | custom-call | tf_op jit(solution)/shard_map/pallas_call | solution.py:1015
  330.5 8.5 %shard_map.365 = (bf16[2048,2304]{1,0:T(8,128)(2,1)}, f32[2048,128]{1,0:T(8,128)}) custom-call(bf16[2048,2304]{1,0:T(8,128)(2,1)} %get-tuple-element.135.refs_0_, bf16[2048,2176]{1,0:T(8,128)(2,1)} %all-gather.5.cloned.1.call-done.wa_ref.refs_1_, bf16[2048,528]{1,0:T(8,128)(2,1)} %shard_map.349.refs_2_.refs_5_, ...), custom_call_target="tpu_custom_call", output_to_operand_aliasing={{0}: (0, {})} | custom-call | flops 2147483648 | bytes 8388608 | tf_op jit(solution)/shard_map/pallas_call | solution.py:788
  357.5 6.2 %fusion.13 = bf16[256,2048]{1,0:T(8,128)(2,1)} fusion(bf16[2048,2176]{1,0:T(8,128)(2,1)} %all-gather.5.cloned.1.call-done.wa_ref.refs_1_, bf16[512,1664]{1,0:T(8,128)(2,1)S(1)} %fusion.48), kind=kOutput, calls=%fused_computation.11 | convolution fusion | flops 1745354752 | bytes 8716288 | tf_op jit(solution)/shard_map/dot_general | solution.py:885
  364.1 4.2 collective-permute-start.66
  376.4 4.2 collective-permute-start.47
  382.6 5.2 %collective-permute-done.47 = bf16[256,512]{1,0:T(8,128)(2,1)S(1)} collective-permute-done((bf16[256,512]{1,0:T(8,128)(2,1)S(1)}, bf16[256,512]{1,0:T(8,128)(2,1)S(1)}, u32[]{:S(2)}, u32[]{:S(2)}) %collective-permute-start.47) | collective-permute-done | bytes 262176 | tf_op jit(solution)/shard_map/ppermute | solution.py:829
  392.8 4.0 convolution_convert_fusion.2
  416.6 5.4 %collective-permute-done.51 = bf16[256,512]{1,0:T(8,128)(2,1)} collective-permute-done((bf16[256,512]{1,0:T(8,128)(2,1)}, bf16[256,512]{1,0:T(8,128)(2,1)}, u32[]{:S(2)}, u32[]{:S(2)}) %collective-permute-start.51) | collective-permute-done | bytes 262176 | tf_op jit(solution)/shard_map/ppermute | solution.py:829
  (384 shorter events, 205.7 us)
Async XLA Ops:
  7.2 83.3 %all-gather.5.cloned.1.call-start = ((), (), s32[]{:S(2)}) async-start(), calls=%async_computation.3 | async-start | bytes 9469952 | tf_op jit(solution)/shard_map/all_gather | solution.py:843
  13.4 185.6 %all-gather.3.cloned.1.call-start = ((), (), s32[]{:S(2)}) async-start(), calls=%async_computation.2 | async-start | bytes 10027008 | tf_op jit(solution)/shard_map/all_gather | solution.py:843
  18.8 394.7 %reduce-scatter.5.cloned.1.call-start = ((), (), s32[]{:S(2)}) async-start(), calls=%async_computation.5 | async-start | bytes 10027008 | tf_op jit(solution)/shard_map/reduce_scatter | solution.py:847
  31.5 11.3 %collective-permute-start.6 = (bf16[256,512]{1,0:T(8,128)(2,1)S(1)}, bf16[256,512]{1,0:T(8,128)(2,1)S(1)}, u32[]{:S(2)}, u32[]{:S(2)}) collective-permute-start(bf16[256,512]{1,0:T(8,128)(2,1)S(1)} %copy-done.42), channel_id=1, source_target_pairs={{0,1},{1,2},{2,3},{3,0},{4,5},{5,6},{6,7},{7,4},{8,9},{9,10},{10,1... | collective-permute-start | bytes 786440 | tf_op jit(solution)/shard_map/ppermute | solution.py:829
  31.6 11.3 %collective-permute-start.8 = (bf16[256,512]{1,0:T(8,128)(2,1)S(1)}, bf16[256,512]{1,0:T(8,128)(2,1)S(1)}, u32[]{:S(2)}, u32[]{:S(2)}) collective-permute-start(bf16[256,512]{1,0:T(8,128)(2,1)S(1)} %copy-done.42), channel_id=1, source_target_pairs={{0,3},{1,0},{2,1},{3,2},{4,7},{5,4},{6,5},{7,6},{8,11},{9,8},{10,9... | collective-permute-start | bytes 786440 | tf_op jit(solution)/shard_map/ppermute | solution.py:829
  42.7 12.8 %collective-permute-start.4 = (bf16[256,2048]{1,0:T(8,128)(2,1)}, bf16[256,2048]{1,0:T(8,128)(2,1)S(1)}, u32[]{:S(2)}, u32[]{:S(2)}) collective-permute-start(bf16[256,2048]{1,0:T(8,128)(2,1)} %get-tuple-element.100.refs_0_), channel_id=1, source_target_pairs={{0,4},{4,0},{8,12},{12,8},{16,20},{20,16},{24,28},{28,24},{32,36},... | collective-permute-start | bytes 3145736 | tf_op jit(solution)/shard_map/ppermute | solution.py:813
  56.4 10.7 %collective-permute-start.5 = (bf16[16,2048]{1,0:T(8,128)(2,1)S(1)}, bf16[16,2048]{1,0:T(8,128)(2,1)S(1)}, u32[]{:S(2)}, u32[]{:S(2)}) collective-permute-start(bf16[16,2048]{1,0:T(8,128)(2,1)S(1)} %slice_select_fusion), channel_id=1, source_target_pairs={{0,8},{4,12},{8,16},{12,20},{16,24},{20,28},{24,32},{28,36},{32,40... | collective-permute-start | bytes 196616 | tf_op jit(solution)/shard_map/ppermute | solution.py:834
  111.3 10.9 %collective-permute-start.13 = (bf16[2,128,384]{2,1,0:T(8,128)(2,1)}, bf16[2,128,384]{2,1,0:T(8,128)(2,1)S(1)}, u32[]{:S(2)}, u32[]{:S(2)}) collective-permute-start(bf16[2,128,384]{2,1,0:T(8,128)(2,1)} %get-tuple-element.110.refs_0_), channel_id=1, source_target_pairs={{0,8},{4,12},{8,16},{12,20},{16,24},{20,28},{24,0},{28,4},{32,40},... | collective-permute-start | bytes 589832 | tf_op jit(solution)/shard_map/ppermute | solution.py:813
  131.6 11.6 %collective-permute-start.19 = (bf16[2,128,384]{2,1,0:T(8,128)(2,1)}, bf16[2,128,384]{2,1,0:T(8,128)(2,1)S(1)}, u32[]{:S(2)}, u32[]{:S(2)}) collective-permute-start(bf16[2,128,384]{2,1,0:T(8,128)(2,1)} %shard_map.354.refs_5_), channel_id=1, source_target_pairs={{0,96},{4,100},{8,104},{12,108},{16,112},{20,116},{24,120},{28,124... | collective-permute-start | bytes 589832 | tf_op jit(solution)/shard_map/ppermute | solution.py:813
  134.5 12.4 %collective-permute-start.17 = (bf16[2,128,384]{2,1,0:T(8,128)(2,1)}, bf16[2,128,384]{2,1,0:T(8,128)(2,1)S(1)}, u32[]{:S(2)}, u32[]{:S(2)}) collective-permute-start(bf16[2,128,384]{2,1,0:T(8,128)(2,1)} %shard_map.354.refs_5_), channel_id=1, source_target_pairs={{0,32},{4,36},{8,40},{12,44},{16,48},{20,52},{24,56},{28,60},{32,6... | collective-permute-start | bytes 589832 | tf_op jit(solution)/shard_map/ppermute | solution.py:813
  169.5 10.7 %collective-permute-start.22 = (bf16[256,512]{1,0:T(8,128)(2,1)S(1)}, bf16[256,512]{1,0:T(8,128)(2,1)S(1)}, u32[]{:S(2)}, u32[]{:S(2)}) collective-permute-start(bf16[256,512]{1,0:T(8,128)(2,1)S(1)} %get-tuple-element.191), channel_id=1, source_target_pairs={{0,2},{1,3},{2,0},{3,1},{4,6},{5,7},{6,4},{7,5},{8,10},{9,11},{10,... | collective-permute-start | bytes 786440 | tf_op jit(solution)/shard_map/ppermute | solution.py:829
  172.6 12.9 %collective-permute-start.24 = (bf16[256,512]{1,0:T(8,128)(2,1)S(1)}, bf16[256,512]{1,0:T(8,128)(2,1)S(1)}, u32[]{:S(2)}, u32[]{:S(2)}) collective-permute-start(bf16[256,512]{1,0:T(8,128)(2,1)S(1)} %get-tuple-element.192), channel_id=1, source_target_pairs={{0,3},{1,0},{2,1},{3,2},{4,7},{5,4},{6,5},{7,6},{8,11},{9,8},{10,9... | collective-permute-start | bytes 786440 | tf_op jit(solution)/shard_map/ppermute | solution.py:829
  173.8 11.7 %collective-permute-start.23 = (bf16[256,512]{1,0:T(8,128)(2,1)S(1)}, bf16[256,512]{1,0:T(8,128)(2,1)S(1)}, u32[]{:S(2)}, u32[]{:S(2)}) collective-permute-start(bf16[256,512]{1,0:T(8,128)(2,1)S(1)} %get-tuple-element.193), channel_id=1, source_target_pairs={{0,1},{1,2},{2,3},{3,0},{4,5},{5,6},{6,7},{7,4},{8,9},{9,10},{10,1... | collective-permute-start | bytes 786440 | tf_op jit(solution)/shard_map/ppermute | solution.py:829
  228.9 16.0 %collective-permute-start.31 = (bf16[256,512]{1,0:T(8,128)(2,1)S(1)}, bf16[256,512]{1,0:T(8,128)(2,1)S(1)}, u32[]{:S(2)}, u32[]{:S(2)}) collective-permute-start(bf16[256,512]{1,0:T(8,128)(2,1)S(1)} %get-tuple-element.188), channel_id=1, source_target_pairs={{0,2},{1,3},{2,0},{3,1},{4,6},{5,7},{6,4},{7,5},{8,10},{9,11},{10,... | collective-permute-start | bytes 786440 | tf_op jit(solution)/shard_map/ppermute | solution.py:829
  229.9 15.0 %collective-permute-start.33 = (bf16[256,512]{1,0:T(8,128)(2,1)S(1)}, bf16[256,512]{1,0:T(8,128)(2,1)}, u32[]{:S(2)}, u32[]{:S(2)}) collective-permute-start(bf16[256,512]{1,0:T(8,128)(2,1)S(1)} %get-tuple-element.189), channel_id=1, source_target_pairs={{0,3},{1,0},{2,1},{3,2},{4,7},{5,4},{6,5},{7,6},{8,11},{9,8},{10,9... | collective-permute-start | bytes 786440 | tf_op jit(solution)/shard_map/ppermute | solution.py:829
  231.7 13.2 %collective-permute-start.32 = (bf16[256,512]{1,0:T(8,128)(2,1)S(1)}, bf16[256,512]{1,0:T(8,128)(2,1)}, u32[]{:S(2)}, u32[]{:S(2)}) collective-permute-start(bf16[256,512]{1,0:T(8,128)(2,1)S(1)} %get-tuple-element.190), channel_id=1, source_target_pairs={{0,1},{1,2},{2,3},{3,0},{4,5},{5,6},{6,7},{7,4},{8,9},{9,10},{10,1... | collective-permute-start | bytes 786440 | tf_op jit(solution)/shard_map/ppermute | solution.py:829
  246.2 185.0 %reduce-scatter.3.cloned.1.call-start = ((), (), s32[]{:S(2)}) async-start(), calls=%async_computation.4 | async-start | bytes 10027008 | tf_op jit(solution)/shard_map/reduce_scatter | solution.py:847
  282.8 10.9 %collective-permute-start.40 = (bf16[2,128,256]{2,1,0:T(8,128)(2,1)}, bf16[2,128,256]{2,1,0:T(8,128)(2,1)S(1)}, u32[]{:S(2)}, u32[]{:S(2)}) collective-permute-start(bf16[2,128,256]{2,1,0:T(8,128)(2,1)} %get-tuple-element.127.refs_0_.refs_5_), channel_id=1, source_target_pairs={{0,16},{4,20},{8,24},{12,28},{16,0},{20,4},{24,8},{28,12},{32,48},... | collective-permute-start | bytes 393224 | tf_op jit(solution)/shard_map/ppermute | solution.py:813
  283.1 13.1 %collective-permute-start.39 = (bf16[2,128,256]{2,1,0:T(8,128)(2,1)}, bf16[2,128,256]{2,1,0:T(8,128)(2,1)S(1)}, u32[]{:S(2)}, u32[]{:S(2)}) collective-permute-start(bf16[2,128,256]{2,1,0:T(8,128)(2,1)} %get-tuple-element.127.refs_0_.refs_5_), channel_id=1, source_target_pairs={{0,8},{4,12},{8,16},{12,20},{16,24},{20,28},{24,0},{28,4},{32,40},... | collective-permute-start | bytes 393224 | tf_op jit(solution)/shard_map/ppermute | solution.py:813
  299.7 13.4 %collective-permute-start.44 = (bf16[2,128,256]{2,1,0:T(8,128)(2,1)}, bf16[2,128,256]{2,1,0:T(8,128)(2,1)S(1)}, u32[]{:S(2)}, u32[]{:S(2)}) collective-permute-start(bf16[2,128,256]{2,1,0:T(8,128)(2,1)} %shard_map.363), channel_id=1, source_target_pairs={{0,96},{4,100},{8,104},{12,108},{16,112},{20,116},{24,120},{28,124... | collective-permute-start | bytes 393224 | tf_op jit(solution)/shard_map/ppermute | solution.py:813
  299.7 13.4 %collective-permute-start.43 = (bf16[2,128,256]{2,1,0:T(8,128)(2,1)}, bf16[2,128,256]{2,1,0:T(8,128)(2,1)S(1)}, u32[]{:S(2)}, u32[]{:S(2)}) collective-permute-start(bf16[2,128,256]{2,1,0:T(8,128)(2,1)} %shard_map.363), channel_id=1, source_target_pairs={{0,64},{4,68},{8,72},{12,76},{16,80},{20,84},{24,88},{28,92},{32,9... | collective-permute-start | bytes 393224 | tf_op jit(solution)/shard_map/ppermute | solution.py:813
  300.2 13.0 %collective-permute-start.42 = (bf16[2,128,256]{2,1,0:T(8,128)(2,1)}, bf16[2,128,256]{2,1,0:T(8,128)(2,1)S(1)}, u32[]{:S(2)}, u32[]{:S(2)}) collective-permute-start(bf16[2,128,256]{2,1,0:T(8,128)(2,1)} %shard_map.363), channel_id=1, source_target_pairs={{0,32},{4,36},{8,40},{12,44},{16,48},{20,52},{24,56},{28,60},{32,6... | collective-permute-start | bytes 393224 | tf_op jit(solution)/shard_map/ppermute | solution.py:813
  352.6 11.1 %collective-permute-start.63 = (f32[102,128]{1,0:T(8,128)S(1)}, f32[102,128]{1,0:T(8,128)S(1)}, u32[]{:S(2)}, u32[]{:S(2)}) collective-permute-start(f32[102,128]{1,0:T(8,128)S(1)} %fusion.62), channel_id=1, source_target_pairs={{0,24},{4,28},{8,0},{12,4},{16,8},{20,12},{24,16},{28,20},{32,56},... | collective-permute-start | bytes 156680 | tf_op jit(solution)/shard_map/ppermute | solution.py:813
  363.7 12.4 %collective-permute-start.46 = (bf16[256,2048]{1,0:T(8,128)(2,1)}, bf16[256,2048]{1,0:T(8,128)(2,1)S(1)}, u32[]{:S(2)}, u32[]{:S(2)}) collective-permute-start(bf16[256,2048]{1,0:T(8,128)(2,1)} %fusion.13), channel_id=1, source_target_pairs={{0,4},{4,0},{8,12},{12,8},{16,20},{20,16},{24,28},{28,24},{32,36},... | collective-permute-start | bytes 3145736 | tf_op jit(solution)/shard_map/ppermute | solution.py:813
  376.4 11.4 %collective-permute-start.47 = (bf16[256,512]{1,0:T(8,128)(2,1)S(1)}, bf16[256,512]{1,0:T(8,128)(2,1)S(1)}, u32[]{:S(2)}, u32[]{:S(2)}) collective-permute-start(bf16[256,512]{1,0:T(8,128)(2,1)S(1)} %get-tuple-element.185), channel_id=1, source_target_pairs={{0,2},{1,3},{2,0},{3,1},{4,6},{5,7},{6,4},{7,5},{8,10},{9,11},{10,... | collective-permute-start | bytes 786440 | tf_op jit(solution)/shard_map/ppermute | solution.py:829
  380.5 10.7 %collective-permute-start.49 = (bf16[256,512]{1,0:T(8,128)(2,1)S(1)}, bf16[256,512]{1,0:T(8,128)(2,1)S(1)}, u32[]{:S(2)}, u32[]{:S(2)}) collective-permute-start(bf16[256,512]{1,0:T(8,128)(2,1)S(1)} %get-tuple-element.186), channel_id=1, source_target_pairs={{0,3},{1,0},{2,1},{3,2},{4,7},{5,4},{6,5},{7,6},{8,11},{9,8},{10,9... | collective-permute-start | bytes 786440 | tf_op jit(solution)/shard_map/ppermute | solution.py:829
  380.6 11.8 %collective-permute-start.48 = (bf16[256,512]{1,0:T(8,128)(2,1)S(1)}, bf16[256,512]{1,0:T(8,128)(2,1)S(1)}, u32[]{:S(2)}, u32[]{:S(2)}) collective-permute-start(bf16[256,512]{1,0:T(8,128)(2,1)S(1)} %get-tuple-element.187), channel_id=1, source_target_pairs={{0,1},{1,2},{2,3},{3,0},{4,5},{5,6},{6,7},{7,4},{8,9},{9,10},{10,1... | collective-permute-start | bytes 786440 | tf_op jit(solution)/shard_map/ppermute | solution.py:829
  396.8 12.9 %collective-permute-start.50 = (bf16[256,2048]{1,0:T(8,128)(2,1)}, bf16[256,2048]{1,0:T(8,128)(2,1)S(1)}, u32[]{:S(2)}, u32[]{:S(2)}) collective-permute-start(bf16[256,2048]{1,0:T(8,128)(2,1)} %convolution_convert_fusion.2), channel_id=1, source_target_pairs={{0,4},{4,0},{8,12},{12,8},{16,20},{20,16},{24,28},{28,24},{32,36},... | collective-permute-start | bytes 3145736 | tf_op jit(solution)/shard_map/ppermute | solution.py:813
  410.9 11.1 %collective-permute-start.51 = (bf16[256,512]{1,0:T(8,128)(2,1)}, bf16[256,512]{1,0:T(8,128)(2,1)}, u32[]{:S(2)}, u32[]{:S(2)}) collective-permute-start(bf16[256,512]{1,0:T(8,128)(2,1)} %get-tuple-element.182), channel_id=1, source_target_pairs={{0,2},{1,3},{2,0},{3,1},{4,6},{5,7},{6,4},{7,5},{8,10},{9,11},{10,... | collective-permute-start | bytes 786440 | tf_op jit(solution)/shard_map/ppermute | solution.py:829
  411.5 13.7 %collective-permute-start.53 = (bf16[256,512]{1,0:T(8,128)(2,1)}, bf16[256,512]{1,0:T(8,128)(2,1)}, u32[]{:S(2)}, u32[]{:S(2)}) collective-permute-start(bf16[256,512]{1,0:T(8,128)(2,1)} %get-tuple-element.183), channel_id=1, source_target_pairs={{0,3},{1,0},{2,1},{3,2},{4,7},{5,4},{6,5},{7,6},{8,11},{9,8},{10,9... | collective-permute-start | bytes 786440 | tf_op jit(solution)/shard_map/ppermute | solution.py:829
  413.2 12.1 %collective-permute-start.52 = (bf16[256,512]{1,0:T(8,128)(2,1)S(1)}, bf16[256,512]{1,0:T(8,128)(2,1)}, u32[]{:S(2)}, u32[]{:S(2)}) collective-permute-start(bf16[256,512]{1,0:T(8,128)(2,1)S(1)} %get-tuple-element.184), channel_id=1, source_target_pairs={{0,1},{1,2},{2,3},{3,0},{4,5},{5,6},{6,7},{7,4},{8,9},{9,10},{10,1... | collective-permute-start | bytes 786440 | tf_op jit(solution)/shard_map/ppermute | solution.py:829
  414.5 12.9 %collective-permute-start.67 = (bf16[64,2304]{1,0:T(8,128)(2,1)S(1)}, bf16[64,2304]{1,0:T(8,128)(2,1)S(1)}, u32[]{:S(2)}, u32[]{:S(2)}) collective-permute-start(bf16[64,2304]{1,0:T(8,128)(2,1)S(1)} %constant_dynamic-slice_fusion), channel_id=1, source_target_pairs={{0,4},{4,0},{8,12},{12,8},{16,20},{20,16},{24,28},{28,24},{32,36},... | collective-permute-start | bytes 884744 | tf_op jit(solution)/shard_map/ppermute | solution.py:813
  (116 other events, 963.1 us)
Sparse Core Ops, SparseCore 0:
  13.6 76.9 all-gather.4
  92.7 83.6 all-gather.2
  246.3 90.9 reduce-scatter.4
  341.1 90.0 reduce-scatter.2
